TPU v7x, 256 devices: a whole 4x4x8 slice. The times are simulated.
256 devices in a mesh: phi: 32 (over z, y_hi, core), row: 8 (over x, y_lo).
Axes of the slice: x: 4, y: 4 (y_hi: 2, y_lo: 2; y = y_hi * 2 + y_lo), z: 8, core: 2. Of those that a mesh axis runs over, the one named last changes fastest.
Arguments:
- gas_density: float32 [8, 128, 4096], P(None, 'row', 'phi'), may hold values from 0.25 to 4
- gas_velocity: float32 [3, 8, 128, 4096], P(None, None, 'row', 'phi'), may hold values from -1 to 1
- orbital_offsets: int32 [2, 128], P(None, 'row'), may hold values from 0 to 4095
- residual_courant: float32 [2, 128], P(None, 'row'), may hold values from -0.45 to 0.45
- dust_mass: float32 [4, 8, 128, 4096], P(None, None, 'row', 'phi'), may hold values from 0.02 to 0.2
- dust_stop: float32 [4, 8, 128, 4096], P(None, None, 'row', 'phi'), may hold values from 0.2 to 5
- dust_velocity: float32 [2, 4, 8, 128, 4096], P(None, None, None, 'row', 'phi'), may hold values from -1 to 1
- occupancy: int32 [8, 128, 4096], P(None, 'row', 'phi'), may hold values from 0 to 4, as said below
- move_count: int32 [8, 128, 4096], P(None, 'row', 'phi'), may hold values from 0 to 4, as said below
- dest_tile: int32 [8, 128, 4096], P(None, 'row', 'phi'), may hold values from 0 to 7, as said below
Outputs:
- new_density: float32 [8, 128, 4096], P(None, 'row', 'phi')
- new_velocity: float32 [3, 8, 128, 4096], P(None, None, 'row', 'phi')
- dust_grid: float32 [3, 8, 128, 4096], P(None, None, 'row', 'phi')
Inputs may be any that keep to these rules, and one draw needn't show every extreme that they name: The block of each cell holds its live particles in slots 0 .. occupancy - 1; the other slots hold no particle. `move_count`: at most the cell's occupancy. In every device block (radial tile t, azimuthal cells [p * 128, (p + 1) * 128), all vertical cells) exactly 2560 cells have migrants: exactly 1024 of them go to one destination tile, which may differ from block to block, and exactly 256 to each other tile except that one and the block's own tile. `dest_tile`: where move_count is positive, another tile than the cell's own; where it is 0, the cell's own tile.
All inputs are finite; a program needn't handle non-finite values.
Results may differ from a plain program's by a relative error of at most 0.0003.
Values sent between devices are 32-bit elements; how exact they have to be, the bound alone decides.
A program may use at most 64 MiB of HBM per device.

v0:
```python
import jax
import jax.numpy as jnp
from jax import lax
from jax.sharding import PartitionSpec as P

K = 4
STEPS = 2


twelfth = 1.0 / 12.0
radial_rate = 0.15
density_floor = 0.5
lane_width = 128


def shifted(value, axis, steps):
    count = lax.axis_size(axis)
    pairs = [(source, (source + steps) % count) for source in range(count)]
    return lax.ppermute(value, axis, pairs)


def extended(array, sides, width, wrap):
    for axis, dim in sides:
        size, length = (lax.axis_size(axis), array.shape[dim])
        up = [(i, (i + 1) % size) for i in range(size if wrap else size - 1)]
        down = [(j, i) for i, j in up]
        last = lax.slice_in_dim(array, length - width, length, axis=dim)
        first = lax.slice_in_dim(array, 0, width, axis=dim)
        before = lax.ppermute(last, axis, up)
        after = lax.ppermute(first, axis, down)
        array = jnp.concatenate([before, array, after], axis=dim)
    return array


def ppm_sweep(padded, courant, sweep_axis):
    length = padded.shape[sweep_axis] - 6

    def window(offset, extent):
        return lax.slice_in_dim(padded, offset, offset + extent, axis=sweep_axis)

    face_values = (
        7.0 * (window(1, length + 3) + window(2, length + 3))
        - (window(0, length + 3) + window(3, length + 3))
    ) * twelfth
    left_face = lax.slice_in_dim(face_values, 0, length + 2, axis=sweep_axis)
    right_face = lax.slice_in_dim(face_values, 1, length + 3, axis=sweep_axis)
    centre = window(2, length + 2)
    face_jump = right_face - left_face
    curvature = 6.0 * (centre - 0.5 * (left_face + right_face))

    def faces_from(values, offset):
        return lax.slice_in_dim(values, offset, offset + length + 1, axis=sweep_axis)

    from_left = courant * (
        faces_from(right_face, 0)
        - 0.5
        * courant
        * (faces_from(face_jump, 0) - (1.0 - 2.0 * courant / 3.0) * faces_from(curvature, 0))
    )
    from_right = courant * (
        faces_from(left_face, 1)
        - 0.5
        * courant
        * (faces_from(face_jump, 1) + (1.0 + 2.0 * courant / 3.0) * faces_from(curvature, 1))
    )
    fluxes = jnp.where(courant >= 0.0, from_left, from_right)
    interior = window(3, length)
    return interior - (
        lax.slice_in_dim(fluxes, 1, length + 1, axis=sweep_axis)
        - lax.slice_in_dim(fluxes, 0, length, axis=sweep_axis)
    )


def apply_drag(gas_state, radial_dust, azimuth_dust, dust_stop, dust_mass, live_slots):
    floored = jnp.maximum(gas_state[0], density_floor)
    coupling = floored[None] * dust_stop
    fresh_radial = (radial_dust + coupling * gas_state[1][None]) / (1.0 + coupling)
    fresh_azimuth = (azimuth_dust + coupling * gas_state[2][None]) / (1.0 + coupling)
    fresh_radial = jnp.where(live_slots, fresh_radial, radial_dust)
    fresh_azimuth = jnp.where(live_slots, fresh_azimuth, azimuth_dust)
    radial_kick = jnp.sum(
        jnp.where(live_slots, dust_mass * (fresh_radial - radial_dust), 0.0), axis=0
    )
    azimuth_kick = jnp.sum(
        jnp.where(live_slots, dust_mass * (fresh_azimuth - azimuth_dust), 0.0), axis=0
    )
    gas_state = jnp.stack(
        [
            gas_state[0],
            gas_state[1] - radial_kick / floored,
            gas_state[2] - azimuth_kick / floored,
            gas_state[3],
        ]
    )
    return (gas_state, fresh_radial, fresh_azimuth)


def deposit(slot_mask, dust_mass, radial_dust, azimuth_dust):
    weighted = jnp.where(slot_mask, dust_mass, 0.0)
    return jnp.stack(
        [
            jnp.sum(weighted, axis=0),
            jnp.sum(weighted * radial_dust, axis=0),
            jnp.sum(weighted * azimuth_dust, axis=0),
        ]
    )


def spread(values, slots, length):
    channels = values.shape[0]
    high_count = -(-length // lane_width)
    high_part = slots // lane_width
    low_part = slots % lane_width
    high_hot = (high_part[None, :] == jnp.arange(high_count, dtype=jnp.int32)[:, None]).astype(
        jnp.float32
    )
    low_hot = (low_part[:, None] == jnp.arange(lane_width, dtype=jnp.int32)[None, :]).astype(
        jnp.float32
    )
    left_side = (values[:, None, :] * high_hot[None]).reshape(
        channels * high_count, values.shape[1]
    )
    summed = jnp.dot(
        left_side, low_hot, precision=lax.Precision.HIGHEST, preferred_element_type=jnp.float32
    )
    return summed.reshape(channels, high_count * lane_width)


def shift_by_hops(gas_state, offsets, phi_cells, loop_devices):
    whole_hops = offsets // phi_cells
    remainder = offsets % phi_cells
    for bit_number in range((loop_devices - 1).bit_length()):
        hopped = shifted(gas_state, "phi", 1 << bit_number)
        chosen = whole_hops >> bit_number & 1 == 1
        gas_state = jnp.where(chosen[None, None, :, None], hopped, gas_state)
    previous = shifted(gas_state, "phi", 1)
    joined = jnp.concatenate([previous, gas_state], axis=3)
    for bit_number in range((phi_cells - 1).bit_length()):
        amount = 1 << bit_number
        moved = jnp.concatenate(
            [jnp.zeros_like(joined[..., :amount]), joined[..., :-amount]], axis=3
        )
        chosen = remainder >> bit_number & 1 == 1
        joined = jnp.where(chosen[None, None, :, None], moved, joined)
    return joined[..., phi_cells:]


def body(
    gas_density,
    gas_velocity,
    orbital_offsets,
    residual_courant,
    dust_mass,
    dust_stop,
    dust_velocity,
    occupancy,
    move_count,
    dest_tile,
):
    gas_state = jnp.concatenate([gas_density[None], gas_velocity], axis=0)
    phi_cells = gas_state.shape[3]
    radial_cells = gas_state.shape[2]
    loop_devices = lax.axis_size("phi")
    row_devices = lax.axis_size("row")
    row_place = lax.axis_index("row")
    at_start = row_place == 0
    at_end = row_place == row_devices - 1
    slot_index = jnp.arange(K, dtype=jnp.int32)[:, None, None, None]
    live_slots = slot_index < occupancy[None]
    radial_dust = dust_velocity[0]
    azimuth_dust = dust_velocity[1]
    for step_index in range(STEPS):
        offsets = orbital_offsets[step_index]
        gas_state = shift_by_hops(gas_state, offsets, phi_cells, loop_devices)
        wrapped = extended(gas_state, (("phi", 3),), 3, True)
        gas_state = ppm_sweep(wrapped, residual_courant[step_index][None, None, :, None], 3)
        received = extended(gas_state, (("row", 2),), 3, False)
        rim_shape = gas_state.shape[:2] + (3, phi_cells)
        low_rim = jnp.where(
            at_start, jnp.broadcast_to(gas_state[:, :, :1], rim_shape), received[:, :, :3]
        )
        high_rim = jnp.where(
            at_end,
            jnp.broadcast_to(gas_state[:, :, -1:], rim_shape),
            received[:, :, radial_cells + 3 :],
        )
        radial_padded = jnp.concatenate([low_rim, gas_state, high_rim], axis=2)
        radial_speed = radial_padded[1]
        courant = (
            radial_rate
            * (radial_speed[:, 2 : radial_cells + 3] + radial_speed[:, 3 : radial_cells + 4])
        )[None]
        gas_state = ppm_sweep(radial_padded, courant, 2)
        gas_state, radial_dust, azimuth_dust = apply_drag(
            gas_state, radial_dust, azimuth_dust, dust_stop, dust_mass, live_slots
        )
    leaving = slot_index >= (occupancy - move_count)[None]
    staying = jnp.logical_and(live_slots, jnp.logical_not(leaving))
    moving = jnp.logical_and(live_slots, leaving)
    kept_grid = deposit(staying, dust_mass, radial_dust, azimuth_dust)
    migrating = deposit(moving, dust_mass, radial_dust, azimuth_dust)
    tile_cells = occupancy.size
    box_slots = tile_cells // 16
    list_length = box_slots + (row_devices - 2) * (box_slots // 4)
    migrating_flat = migrating.reshape(3, tile_cells)
    dest_flat = dest_tile.reshape(tile_cells)
    moving_flat = move_count.reshape(tile_cells) > 0
    cell_numbers = jnp.arange(tile_cells, dtype=jnp.int32)
    list_rank = jnp.cumsum(moving_flat.astype(jnp.int32)) - 1
    list_slot = jnp.where(moving_flat, list_rank, list_length)
    cell_codes = (dest_flat * tile_cells + cell_numbers).astype(jnp.float32)
    code_float = spread(cell_codes[None], list_slot, list_length)[0]
    code_list = (code_float + 0.5).astype(jnp.int32)
    value_list = spread(migrating_flat, list_slot, list_length)
    all_codes, all_values = (
        lax.all_gather(code_list, "row", axis=0, tiled=True),
        lax.all_gather(value_list, "row", axis=1, tiled=True),
    )
    for_here = all_codes // tile_cells == row_place
    target_cell = jnp.where(for_here, all_codes % tile_cells, tile_cells)
    arrived = spread(all_values, target_cell, tile_cells)
    dust_grid = (kept_grid.reshape(3, tile_cells) + arrived).reshape(kept_grid.shape)
    return (gas_state[0], gas_state[1:], dust_grid)


def solution(mesh):
    return jax.shard_map(
        body,
        mesh=mesh,
        in_specs=(
            P(None, "row", "phi"),
            P(None, None, "row", "phi"),
            P(None, "row"),
            P(None, "row"),
            P(None, None, "row", "phi"),
            P(None, None, "row", "phi"),
            P(None, None, None, "row", "phi"),
            P(None, "row", "phi"),
            P(None, "row", "phi"),
            P(None, "row", "phi"),
        ),
        out_specs=(P(None, "row", "phi"), P(None, None, "row", "phi"), P(None, None, "row", "phi")),
        check_vma=False,
    )
```

profile of v0, /device:TPU:8, one launch (start us, length us, event | category | flops | bytes accessed | tf_op | source)
XLA Modules:
  0.0 275.5 jit_solution(669070630443404621)
XLA Ops:
  0.6 1.0 pad_maximum_fusion.6
  1.7 0.8 and_compare_fusion.23
  2.5 0.8 and_compare_fusion.16
  3.3 9.5 %collective-permute-done = f32[4,8,16,128]{3,2,1,0:T(8,128)S(1)} collective-permute-done((f32[4,8,16,128]{3,2,1,0:T(8,128)S(1)}, f32[4,8,16,128]{3,2,1,0:T(8,128)S(1)}, u32[]{:S(2)}, u32[]{:S(2)}) %collective-permute-start) | collective-permute-done | bytes 262176 | tf_op jit(solution)/shard_map/ppermute | solution.py:19
  12.8 1.0 broadcast_select_fusion
  13.9 12.0 %collective-permute-done.1 = f32[4,8,16,128]{3,2,1,0:T(8,128)S(1)} collective-permute-done((f32[4,8,16,128]{3,2,1,0:T(8,128)S(1)}, f32[4,8,16,128]{3,2,1,0:T(8,128)S(1)}, u32[]{:S(2)}, u32[]{:S(2)}) %collective-permute-start.1) | collective-permute-done | bytes 262176 | tf_op jit(solution)/shard_map/ppermute | solution.py:19
  26.1 9.4 %collective-permute-done.2 = f32[4,8,16,128]{3,2,1,0:T(8,128)S(1)} collective-permute-done((f32[4,8,16,128]{3,2,1,0:T(8,128)S(1)}, f32[4,8,16,128]{3,2,1,0:T(8,128)S(1)}, u32[]{:S(2)}, u32[]{:S(2)}) %collective-permute-start.2) | collective-permute-done | bytes 262176 | tf_op jit(solution)/shard_map/ppermute | solution.py:19
  35.7 0.9 fusion.115
  36.5 13.7 %collective-permute-done.3 = f32[4,8,16,128]{3,2,1,0:T(8,128)S(1)} collective-permute-done((f32[4,8,16,128]{3,2,1,0:T(8,128)S(1)}, f32[4,8,16,128]{3,2,1,0:T(8,128)S(1)}, u32[]{:S(2)}, u32[]{:S(2)}) %collective-permute-start.3) | collective-permute-done | bytes 262176 | tf_op jit(solution)/shard_map/ppermute | solution.py:19
  50.3 7.0 %collective-permute-start.4 = (f32[4,8,16,128]{3,2,1,0:T(8,128)S(1)}, f32[4,8,16,128]{3,2,1,0:T(8,128)S(1)}, u32[]{:S(2)}, u32[]{:S(2)}) collective-permute-start(f32[4,8,16,128]{3,2,1,0:T(8,128)S(1)} %broadcast_select_fusion.3), channel_id=1, source_target_pairs={{0,128},{8,136},{16,144},{24,152},{32,160},{40,168},{48,176},{56,1... | collective-permute-start | bytes 786440 | tf_op jit(solution)/shard_map/ppermute | solution.py:19
  57.4 0.8 broadcast_compare_fusion.4
  58.7 5.8 %collective-permute-done.4 = f32[4,8,16,128]{3,2,1,0:T(8,128)S(1)} collective-permute-done((f32[4,8,16,128]{3,2,1,0:T(8,128)S(1)}, f32[4,8,16,128]{3,2,1,0:T(8,128)S(1)}, u32[]{:S(2)}, u32[]{:S(2)}) %collective-permute-start.4) | collective-permute-done | bytes 262176 | tf_op jit(solution)/shard_map/ppermute | solution.py:19
  64.8 9.4 %collective-permute-done.5 = f32[4,8,16,128]{3,2,1,0:T(8,128)S(1)} collective-permute-done((f32[4,8,16,128]{3,2,1,0:T(8,128)S(1)}, f32[4,8,16,128]{3,2,1,0:T(8,128)S(1)}, u32[]{:S(2)}, u32[]{:S(2)}) %collective-permute-start.5) | collective-permute-done | bytes 262176 | tf_op jit(solution)/shard_map/ppermute | solution.py:19
  76.0 5.3 %collective-permute-start.7 = (f32[4,8,16,3]{3,2,1,0:T(8,128)S(1)}, f32[4,8,16,3]{3,2,1,0:T(8,128)S(1)}, u32[]{:S(2)}, u32[]{:S(2)}) collective-permute-start(f32[4,8,16,3]{3,2,1,0:T(8,128)S(1)} %get-tuple-element.42), channel_id=1, source_target_pairs={{8,0},{16,8},{24,16},{32,24},{40,32},{48,40},{56,48},{64,56},{72,6... | collective-permute-start | bytes 18440 | tf_op jit(solution)/shard_map/ppermute | solution.py:30
  81.4 4.0 %collective-permute-done.6 = f32[4,8,16,3]{3,2,1,0:T(8,128)S(1)} collective-permute-done((f32[4,8,16,3]{3,2,1,0:T(8,128)S(1)}, f32[4,8,16,3]{3,2,1,0:T(8,128)S(1)}, u32[]{:S(2)}, u32[]{:S(2)}) %collective-permute-start.6) | collective-permute-done | bytes 6176 | tf_op jit(solution)/shard_map/ppermute | solution.py:29
  85.7 0.5 fusion.56
  86.1 0.3 slice_subtract_fusion.3
  86.5 0.5 fusion.48
  87.2 4.5 %collective-permute-start.8 = (f32[4,8,3,128]{3,2,1,0:T(4,128)S(1)}, f32[4,8,3,128]{3,2,1,0:T(4,128)S(1)}, u32[]{:S(2)}, u32[]{:S(2)}) collective-permute-start(f32[4,8,3,128]{3,2,1,0:T(4,128)S(1)} %get-tuple-element.67), channel_id=1, source_target_pairs={{0,1},{1,2},{2,3},{3,4},{4,5},{5,6},{6,7},{8,9},{9,10},{10,11},{11... | collective-permute-start | bytes 147464 | tf_op jit(solution)/shard_map/ppermute | solution.py:29
  91.7 1.9 collective-permute-start.9
  93.7 5.1 %collective-permute-done.9 = f32[4,8,3,128]{3,2,1,0:T(4,128)S(1)} collective-permute-done((f32[4,8,3,128]{3,2,1,0:T(4,128)S(1)}, f32[4,8,3,128]{3,2,1,0:T(4,128)S(1)}, u32[]{:S(2)}, u32[]{:S(2)}) %collective-permute-start.9) | collective-permute-done | bytes 49184 | tf_op jit(solution)/shard_map/ppermute | solution.py:30
  99.7 0.3 copy-done
  100.6 9.3 %collective-permute-done.10 = f32[4,8,16,128]{3,2,1,0:T(8,128)S(1)} collective-permute-done((f32[4,8,16,128]{3,2,1,0:T(8,128)S(1)}, f32[4,8,16,128]{3,2,1,0:T(8,128)S(1)}, u32[]{:S(2)}, u32[]{:S(2)}) %collective-permute-start.10) | collective-permute-done | bytes 262176 | tf_op jit(solution)/shard_map/ppermute | solution.py:19
  110.3 12.4 %collective-permute-done.11 = f32[4,8,16,128]{3,2,1,0:T(8,128)S(1)} collective-permute-done((f32[4,8,16,128]{3,2,1,0:T(8,128)S(1)}, f32[4,8,16,128]{3,2,1,0:T(8,128)S(1)}, u32[]{:S(2)}, u32[]{:S(2)}) %collective-permute-start.11) | collective-permute-done | bytes 262176 | tf_op jit(solution)/shard_map/ppermute | solution.py:19
  123.1 9.1 %collective-permute-done.12 = f32[4,8,16,128]{3,2,1,0:T(8,128)S(1)} collective-permute-done((f32[4,8,16,128]{3,2,1,0:T(8,128)S(1)}, f32[4,8,16,128]{3,2,1,0:T(8,128)S(1)}, u32[]{:S(2)}, u32[]{:S(2)}) %collective-permute-start.12) | collective-permute-done | bytes 262176 | tf_op jit(solution)/shard_map/ppermute | solution.py:19
  132.3 3.4 %fusion.21 = s32[20,128]{1,0:T(8,128)S(1)} fusion(s32[16384]{0:T(1024)S(1)} %get-tuple-element.80, f32[20,16384]{1,0:T(8,128)S(1)} %fusion.135), kind=kOutput, calls=%fused_computation.19 | convolution fusion | flops 505418752 | bytes 1386496 | tf_op jit(solution)/shard_map/dot_general | solution.py:123
  135.8 26.2 %all-gather = s32[8,1,2560]{2,1,0:T(1,128)S(1)} all-gather(s32[1,1,2560]{2,1,0:T(1,128)S(1)} %reshape.639), channel_id=1, replica_groups=mesh['phi'=32,'row'=8] {'row'}, dimensions={0}, use_global_device_ids=true | all-gather | bytes 92160 | tf_op jit(solution)/shard_map/all_gather | solution.py:216
  162.0 5.2 %collective-permute-start.14 = (f32[4,8,16,128]{3,2,1,0:T(8,128)S(1)}, f32[4,8,16,128]{3,2,1,0:T(8,128)S(1)}, u32[]{:S(2)}, u32[]{:S(2)}) collective-permute-start(f32[4,8,16,128]{3,2,1,0:T(8,128)S(1)} %broadcast_select_fusion.8), channel_id=1, source_target_pairs={{0,128},{8,136},{16,144},{24,152},{32,160},{40,168},{48,176},{56,1... | collective-permute-start | bytes 786440 | tf_op jit(solution)/shard_map/ppermute | solution.py:19
  167.4 5.0 %collective-permute-done.14 = f32[4,8,16,128]{3,2,1,0:T(8,128)S(1)} collective-permute-done((f32[4,8,16,128]{3,2,1,0:T(8,128)S(1)}, f32[4,8,16,128]{3,2,1,0:T(8,128)S(1)}, u32[]{:S(2)}, u32[]{:S(2)}) %collective-permute-start.14) | collective-permute-done | bytes 262176 | tf_op jit(solution)/shard_map/ppermute | solution.py:19
  172.6 5.1 %compare_convert_fusion = f32[8,16,20480]{2,1,0:T(8,128)} fusion(s32[8,16]{1,0:T(8,128)S(1)} %multiply_add_fusion.2, s32[20480]{0:T(1024)S(1)} %get-tuple-element.77), kind=kLoop, calls=%fused_computation.6 | loop fusion | flops 5242880 | bytes 10568192 | tf_op jit(solution)/shard_map/convert_element_type | solution.py:114
  177.7 4.3 %collective-permute-done.15 = f32[4,8,16,128]{3,2,1,0:T(8,128)S(1)} collective-permute-done((f32[4,8,16,128]{3,2,1,0:T(8,128)S(1)}, f32[4,8,16,128]{3,2,1,0:T(8,128)S(1)}, u32[]{:S(2)}, u32[]{:S(2)}) %collective-permute-start.15) | collective-permute-done | bytes 262176 | tf_op jit(solution)/shard_map/ppermute | solution.py:19
  183.8 5.3 %collective-permute-start.17 = (f32[4,8,16,3]{3,2,1,0:T(8,128)S(1)}, f32[4,8,16,3]{3,2,1,0:T(8,128)S(1)}, u32[]{:S(2)}, u32[]{:S(2)}) collective-permute-start(f32[4,8,16,3]{3,2,1,0:T(8,128)S(1)} %get-tuple-element.38), channel_id=1, source_target_pairs={{8,0},{16,8},{24,16},{32,24},{40,32},{48,40},{56,48},{64,56},{72,6... | collective-permute-start | bytes 18440 | tf_op jit(solution)/shard_map/ppermute | solution.py:30
  189.3 4.0 %collective-permute-done.16 = f32[4,8,16,3]{3,2,1,0:T(8,128)S(1)} collective-permute-done((f32[4,8,16,3]{3,2,1,0:T(8,128)S(1)}, f32[4,8,16,3]{3,2,1,0:T(8,128)S(1)}, u32[]{:S(2)}, u32[]{:S(2)}) %collective-permute-start.16) | collective-permute-done | bytes 6176 | tf_op jit(solution)/shard_map/ppermute | solution.py:29
  193.5 0.5 fusion.43
  194.0 0.3 slice_subtract_fusion.2
  194.4 0.5 fusion.35
  195.0 2.9 %collective-permute-start.18 = (f32[4,8,3,128]{3,2,1,0:T(4,128)S(1)}, f32[4,8,3,128]{3,2,1,0:T(4,128)S(1)}, u32[]{:S(2)}, u32[]{:S(2)}) collective-permute-start(f32[4,8,3,128]{3,2,1,0:T(4,128)S(1)} %get-tuple-element.56), channel_id=1, source_target_pairs={{0,1},{1,2},{2,3},{3,4},{4,5},{5,6},{6,7},{8,9},{9,10},{10,11},{11... | collective-permute-start | bytes 147464 | tf_op jit(solution)/shard_map/ppermute | solution.py:29
  198.0 3.0 %collective-permute-start.19 = (f32[4,8,3,128]{3,2,1,0:T(4,128)S(1)}, f32[4,8,3,128]{3,2,1,0:T(4,128)S(1)}, u32[]{:S(2)}, u32[]{:S(2)}) collective-permute-start(f32[4,8,3,128]{3,2,1,0:T(4,128)S(1)} %get-tuple-element.57), channel_id=1, source_target_pairs={{1,0},{2,1},{3,2},{4,3},{5,4},{6,5},{7,6},{9,8},{10,9},{11,10},{12... | collective-permute-start | bytes 147464 | tf_op jit(solution)/shard_map/ppermute | solution.py:30
  201.2 4.5 %collective-permute-done.19 = f32[4,8,3,128]{3,2,1,0:T(4,128)S(1)} collective-permute-done((f32[4,8,3,128]{3,2,1,0:T(4,128)S(1)}, f32[4,8,3,128]{3,2,1,0:T(4,128)S(1)}, u32[]{:S(2)}, u32[]{:S(2)}) %collective-permute-start.19) | collective-permute-done | bytes 49184 | tf_op jit(solution)/shard_map/ppermute | solution.py:30
  206.7 0.4 multiply_reduce_fusion.2
  207.4 2.6 broadcast_multiply_fusion
  210.0 4.2 %mul.503 = f32[60,16384]{1,0:T(8,128)} reshape(f32[3,20,16384]{2,1,0:T(8,128)} %broadcast_multiply_fusion) | data formatting | bytes 7864320 | tf_op jit(solution)/shard_map/mul | solution.py:120
  214.1 5.7 %fusion.7 = f32[60,128]{1,0:T(8,128)S(1)} fusion(f32[60,16384]{1,0:T(8,128)} %mul.503, s32[16384]{0:T(1024)S(1)} %get-tuple-element.80), kind=kOutput, calls=%fused_computation.9 | convolution fusion | flops 1512046592 | bytes 4028416 | tf_op jit(solution)/shard_map/dot_general | solution.py:123
  219.9 26.7 %all_gather.6 = f32[3,20480]{1,0:T(4,128)S(1)} all-gather(f32[3,2560]{1,0:T(4,128)S(1)} %reshape.637), channel_id=1, replica_groups=mesh['phi'=32,'row'=8] {'row'}, dimensions={1}, use_global_device_ids=true | all-gather | bytes 276480 | tf_op jit(solution)/shard_map/all_gather | solution.py:217
  246.6 0.6 fusion.107
  247.2 7.9 %fusion.133 = f32[3,8,16,20480]{3,2,1,0:T(8,128)S(1)} fusion(f32[8,16,20480]{2,1,0:T(8,128)} %compare_convert_fusion, f32[3,20480]{1,0:T(4,128)S(1)} %all_gather.6), kind=kLoop, calls=%fused_computation.1.clone.clone.clone.2 | loop fusion | flops 7864320 | bytes 42188800 | tf_op jit(solution)/shard_map/dot_general | solution.py:123
  255.2 0.7 pad_maximum_fusion.8
  255.9 19.6 %fusion.13 = f32[3,8,16,128]{3,2,1,0:T(8,128)} fusion(s32[20480]{0:T(1024)S(1)} %get-tuple-element.78, f32[1,8,16,128]{3,2,1,0:T(8,128)S(1)} %bitcast.187, f32[1,8,16,128]{3,2,1,0:T(8,128)S(1)} %bitcast.188, f32[1,8,16,128]{3,2,1,0:T(8,128)S(1)} %bitcast.189, f32[3,8,16,20480]{3,2,1,0:T(8,128)S(1)} %fusion.133), kind=kOutput, calls=%fused_computation.17 | convolution fusion | flops 12082364416 | bytes 31932416 | tf_op jit(solution)/shard_map/dot_general | solution.py:123
  (118 shorter events, 10.2 us)
Async XLA Ops:
  0.6 58.1 %copy-start.6 = (f32[2,16]{1,0:T(2,128)S(1)}, f32[2,16]{1,0:T(2,128)}, u32[]{:S(2)}) copy-start(f32[2,16]{1,0:T(2,128)} %param.13) | copy-start | bytes 388
  1.6 11.2 %collective-permute-start = (f32[4,8,16,128]{3,2,1,0:T(8,128)S(1)}, f32[4,8,16,128]{3,2,1,0:T(8,128)S(1)}, u32[]{:S(2)}, u32[]{:S(2)}) collective-permute-start(f32[4,8,16,128]{3,2,1,0:T(8,128)S(1)} %pad_maximum_fusion.6), channel_id=1, source_target_pairs={{0,8},{8,16},{16,24},{24,32},{32,40},{40,48},{48,56},{56,64},{64,7... | collective-permute-start | bytes 786440 | tf_op jit(solution)/shard_map/ppermute | solution.py:19
  13.8 12.1 %collective-permute-start.1 = (f32[4,8,16,128]{3,2,1,0:T(8,128)S(1)}, f32[4,8,16,128]{3,2,1,0:T(8,128)S(1)}, u32[]{:S(2)}, u32[]{:S(2)}) collective-permute-start(f32[4,8,16,128]{3,2,1,0:T(8,128)S(1)} %broadcast_select_fusion), channel_id=1, source_target_pairs={{0,16},{8,24},{16,32},{24,40},{32,48},{40,56},{48,64},{56,72},{64,... | collective-permute-start | bytes 786440 | tf_op jit(solution)/shard_map/ppermute | solution.py:19
  26.0 9.5 %collective-permute-start.2 = (f32[4,8,16,128]{3,2,1,0:T(8,128)S(1)}, f32[4,8,16,128]{3,2,1,0:T(8,128)S(1)}, u32[]{:S(2)}, u32[]{:S(2)}) collective-permute-start(f32[4,8,16,128]{3,2,1,0:T(8,128)S(1)} %broadcast_select_fusion.1), channel_id=1, source_target_pairs={{0,32},{8,40},{16,48},{24,56},{32,64},{40,72},{48,80},{56,88},{64,... | collective-permute-start | bytes 786440 | tf_op jit(solution)/shard_map/ppermute | solution.py:19
  35.5 14.7 %collective-permute-start.3 = (f32[4,8,16,128]{3,2,1,0:T(8,128)S(1)}, f32[4,8,16,128]{3,2,1,0:T(8,128)S(1)}, u32[]{:S(2)}, u32[]{:S(2)}) collective-permute-start(f32[4,8,16,128]{3,2,1,0:T(8,128)S(1)} %broadcast_select_fusion.2), channel_id=1, source_target_pairs={{0,64},{8,72},{16,80},{24,88},{32,96},{40,104},{48,112},{56,120},{... | collective-permute-start | bytes 786440 | tf_op jit(solution)/shard_map/ppermute | solution.py:19
  50.3 14.2 %collective-permute-start.4 = (f32[4,8,16,128]{3,2,1,0:T(8,128)S(1)}, f32[4,8,16,128]{3,2,1,0:T(8,128)S(1)}, u32[]{:S(2)}, u32[]{:S(2)}) collective-permute-start(f32[4,8,16,128]{3,2,1,0:T(8,128)S(1)} %broadcast_select_fusion.3), channel_id=1, source_target_pairs={{0,128},{8,136},{16,144},{24,152},{32,160},{40,168},{48,176},{56,1... | collective-permute-start | bytes 786440 | tf_op jit(solution)/shard_map/ppermute | solution.py:19
  64.6 9.6 %collective-permute-start.5 = (f32[4,8,16,128]{3,2,1,0:T(8,128)S(1)}, f32[4,8,16,128]{3,2,1,0:T(8,128)S(1)}, u32[]{:S(2)}, u32[]{:S(2)}) collective-permute-start(f32[4,8,16,128]{3,2,1,0:T(8,128)S(1)} %broadcast_select_fusion.4), channel_id=1, source_target_pairs={{0,8},{8,16},{16,24},{24,32},{32,40},{40,48},{48,56},{56,64},{64,7... | collective-permute-start | bytes 786440 | tf_op jit(solution)/shard_map/ppermute | solution.py:19
  75.9 9.5 %collective-permute-start.6 = (f32[4,8,16,3]{3,2,1,0:T(8,128)S(1)}, f32[4,8,16,3]{3,2,1,0:T(8,128)S(1)}, u32[]{:S(2)}, u32[]{:S(2)}) collective-permute-start(f32[4,8,16,3]{3,2,1,0:T(8,128)S(1)} %get-tuple-element.41), channel_id=1, source_target_pairs={{0,8},{8,16},{16,24},{24,32},{32,40},{40,48},{48,56},{56,64},{64,7... | collective-permute-start | bytes 18440 | tf_op jit(solution)/shard_map/ppermute | solution.py:29
  76.0 9.4 %collective-permute-start.7 = (f32[4,8,16,3]{3,2,1,0:T(8,128)S(1)}, f32[4,8,16,3]{3,2,1,0:T(8,128)S(1)}, u32[]{:S(2)}, u32[]{:S(2)}) collective-permute-start(f32[4,8,16,3]{3,2,1,0:T(8,128)S(1)} %get-tuple-element.42), channel_id=1, source_target_pairs={{8,0},{16,8},{24,16},{32,24},{40,32},{48,40},{56,48},{64,56},{72,6... | collective-permute-start | bytes 18440 | tf_op jit(solution)/shard_map/ppermute | solution.py:30
  87.2 6.5 %collective-permute-start.8 = (f32[4,8,3,128]{3,2,1,0:T(4,128)S(1)}, f32[4,8,3,128]{3,2,1,0:T(4,128)S(1)}, u32[]{:S(2)}, u32[]{:S(2)}) collective-permute-start(f32[4,8,3,128]{3,2,1,0:T(4,128)S(1)} %get-tuple-element.67), channel_id=1, source_target_pairs={{0,1},{1,2},{2,3},{3,4},{4,5},{5,6},{6,7},{8,9},{9,10},{10,11},{11... | collective-permute-start | bytes 147464 | tf_op jit(solution)/shard_map/ppermute | solution.py:29
  91.7 7.1 %collective-permute-start.9 = (f32[4,8,3,128]{3,2,1,0:T(4,128)S(1)}, f32[4,8,3,128]{3,2,1,0:T(4,128)S(1)}, u32[]{:S(2)}, u32[]{:S(2)}) collective-permute-start(f32[4,8,3,128]{3,2,1,0:T(4,128)S(1)} %get-tuple-element.68), channel_id=1, source_target_pairs={{1,0},{2,1},{3,2},{4,3},{5,4},{6,5},{7,6},{9,8},{10,9},{11,10},{12... | collective-permute-start | bytes 147464 | tf_op jit(solution)/shard_map/ppermute | solution.py:30
  98.9 1.0 copy-start
  98.9 1.1 copy-start.1
  98.9 1.1 copy-start.2
  98.9 1.2 copy-start.3
  99.2 1.4 copy-start.5
  100.3 9.5 %collective-permute-start.10 = (f32[4,8,16,128]{3,2,1,0:T(8,128)S(1)}, f32[4,8,16,128]{3,2,1,0:T(8,128)S(1)}, u32[]{:S(2)}, u32[]{:S(2)}) collective-permute-start(f32[4,8,16,128]{3,2,1,0:T(8,128)S(1)} %pad_maximum_fusion.7), channel_id=1, source_target_pairs={{0,8},{8,16},{16,24},{24,32},{32,40},{40,48},{48,56},{56,64},{64,7... | collective-permute-start | bytes 786440 | tf_op jit(solution)/shard_map/ppermute | solution.py:19
  109.9 12.8 %collective-permute-start.11 = (f32[4,8,16,128]{3,2,1,0:T(8,128)S(1)}, f32[4,8,16,128]{3,2,1,0:T(8,128)S(1)}, u32[]{:S(2)}, u32[]{:S(2)}) collective-permute-start(f32[4,8,16,128]{3,2,1,0:T(8,128)S(1)} %broadcast_select_fusion.5), channel_id=1, source_target_pairs={{0,16},{8,24},{16,32},{24,40},{32,48},{40,56},{48,64},{56,72},{64,... | collective-permute-start | bytes 786440 | tf_op jit(solution)/shard_map/ppermute | solution.py:19
  122.8 9.3 %collective-permute-start.12 = (f32[4,8,16,128]{3,2,1,0:T(8,128)S(1)}, f32[4,8,16,128]{3,2,1,0:T(8,128)S(1)}, u32[]{:S(2)}, u32[]{:S(2)}) collective-permute-start(f32[4,8,16,128]{3,2,1,0:T(8,128)S(1)} %broadcast_select_fusion.6), channel_id=1, source_target_pairs={{0,32},{8,40},{16,48},{24,56},{32,64},{40,72},{48,80},{56,88},{64,... | collective-permute-start | bytes 786440 | tf_op jit(solution)/shard_map/ppermute | solution.py:19
  132.2 29.7 %collective-permute-start.13 = (f32[4,8,16,128]{3,2,1,0:T(8,128)S(1)}, f32[4,8,16,128]{3,2,1,0:T(8,128)S(1)}, u32[]{:S(2)}, u32[]{:S(2)}) collective-permute-start(f32[4,8,16,128]{3,2,1,0:T(8,128)S(1)} %broadcast_select_fusion.7), channel_id=1, source_target_pairs={{0,64},{8,72},{16,80},{24,88},{32,96},{40,104},{48,112},{56,120},{... | collective-permute-start | bytes 786440 | tf_op jit(solution)/shard_map/ppermute | solution.py:19
  162.0 10.4 %collective-permute-start.14 = (f32[4,8,16,128]{3,2,1,0:T(8,128)S(1)}, f32[4,8,16,128]{3,2,1,0:T(8,128)S(1)}, u32[]{:S(2)}, u32[]{:S(2)}) collective-permute-start(f32[4,8,16,128]{3,2,1,0:T(8,128)S(1)} %broadcast_select_fusion.8), channel_id=1, source_target_pairs={{0,128},{8,136},{16,144},{24,152},{32,160},{40,168},{48,176},{56,1... | collective-permute-start | bytes 786440 | tf_op jit(solution)/shard_map/ppermute | solution.py:19
  172.5 9.5 %collective-permute-start.15 = (f32[4,8,16,128]{3,2,1,0:T(8,128)S(1)}, f32[4,8,16,128]{3,2,1,0:T(8,128)S(1)}, u32[]{:S(2)}, u32[]{:S(2)}) collective-permute-start(f32[4,8,16,128]{3,2,1,0:T(8,128)S(1)} %broadcast_select_fusion.9), channel_id=1, source_target_pairs={{0,8},{8,16},{16,24},{24,32},{32,40},{40,48},{48,56},{56,64},{64,7... | collective-permute-start | bytes 786440 | tf_op jit(solution)/shard_map/ppermute | solution.py:19
  182.7 6.6 %copy-start.4 = (s32[8,16,128]{2,1,0:T(8,128)S(1)}, s32[8,16,128]{2,1,0:T(8,128)}, u32[]{:S(2)}) copy-start(s32[8,16,128]{2,1,0:T(8,128)} %param.18) | copy-start | bytes 196612
  183.7 9.6 %collective-permute-start.16 = (f32[4,8,16,3]{3,2,1,0:T(8,128)S(1)}, f32[4,8,16,3]{3,2,1,0:T(8,128)S(1)}, u32[]{:S(2)}, u32[]{:S(2)}) collective-permute-start(f32[4,8,16,3]{3,2,1,0:T(8,128)S(1)} %get-tuple-element.37), channel_id=1, source_target_pairs={{0,8},{8,16},{16,24},{24,32},{32,40},{40,48},{48,56},{56,64},{64,7... | collective-permute-start | bytes 18440 | tf_op jit(solution)/shard_map/ppermute | solution.py:29
  183.8 9.5 %collective-permute-start.17 = (f32[4,8,16,3]{3,2,1,0:T(8,128)S(1)}, f32[4,8,16,3]{3,2,1,0:T(8,128)S(1)}, u32[]{:S(2)}, u32[]{:S(2)}) collective-permute-start(f32[4,8,16,3]{3,2,1,0:T(8,128)S(1)} %get-tuple-element.38), channel_id=1, source_target_pairs={{8,0},{16,8},{24,16},{32,24},{40,32},{48,40},{56,48},{64,56},{72,6... | collective-permute-start | bytes 18440 | tf_op jit(solution)/shard_map/ppermute | solution.py:30
  195.0 6.2 %collective-permute-start.18 = (f32[4,8,3,128]{3,2,1,0:T(4,128)S(1)}, f32[4,8,3,128]{3,2,1,0:T(4,128)S(1)}, u32[]{:S(2)}, u32[]{:S(2)}) collective-permute-start(f32[4,8,3,128]{3,2,1,0:T(4,128)S(1)} %get-tuple-element.56), channel_id=1, source_target_pairs={{0,1},{1,2},{2,3},{3,4},{4,5},{5,6},{6,7},{8,9},{9,10},{10,11},{11... | collective-permute-start | bytes 147464 | tf_op jit(solution)/shard_map/ppermute | solution.py:29
  198.0 7.7 %collective-permute-start.19 = (f32[4,8,3,128]{3,2,1,0:T(4,128)S(1)}, f32[4,8,3,128]{3,2,1,0:T(4,128)S(1)}, u32[]{:S(2)}, u32[]{:S(2)}) collective-permute-start(f32[4,8,3,128]{3,2,1,0:T(4,128)S(1)} %get-tuple-element.57), channel_id=1, source_target_pairs={{1,0},{2,1},{3,2},{4,3},{5,4},{6,5},{7,6},{9,8},{10,9},{11,10},{12... | collective-permute-start | bytes 147464 | tf_op jit(solution)/shard_map/ppermute | solution.py:30
where the time goes:
time: 277 us; the launch traced here: 276 us
  waiting for transfers between devices  118 us (43%)
  blocking collectives  52.8 us (19%)
  starting transfers between devices  36.4 us (13%)
  other arithmetic  32.6 us (12%)
  matrix products  28.8 us (10%)
  local copies, waits for them, and re-layouts  5.64 us (2%)
    ppermute x12, waiting for transfers between devices, shifted(): return lax.ppermute(value, axis, pairs)  99.9 us
    dot_general x3, matrix products, spread(): jnp.dot(left_side, low_hot, precision=lax.Precision.HIGHEST, preferred_el...  28.8 us
    all_gather x1, blocking collectives, body(): lax.all_gather(value_list, 'row', axis=1, tiled=True)  26.7 us
    all_gather x1, blocking collectives, body(): lax.all_gather(code_list, 'row', axis=0, tiled=True)  26.2 us
    ppermute x4, starting transfers between devices, extended(): after = lax.ppermute(first, axis, down)  15.6 us
    ppermute x12, starting transfers between devices, shifted(): return lax.ppermute(value, axis, pairs)  13.3 us
    ppermute x4, waiting for transfers between devices, extended(): after = lax.ppermute(first, axis, down)  9.55 us
    ppermute x4, waiting for transfers between devices, extended(): before = lax.ppermute(last, axis, up)  8.29 us
  transfers between devices with their start and end apart: 20, of which 16 were waited for; matrix products, arithmetic and copies ran while one was open for 5% of the time, Pallas kernels for 0%

commit v1 on v0

v1 whole, which is shorter than its diff:
```python
import functools

import jax
import jax.numpy as jnp
from jax import lax
from jax.experimental import pallas as pl
from jax.experimental.pallas import tpu as pltpu
from jax.sharding import PartitionSpec as P

K = 4
STEPS = 2
FIELDS = 4
RADIAL = 16
LANES = 128
PAD = 8
SLAB = RADIAL + 2 * PAD

twelfth = 1.0 / 12.0
radial_rate = 0.15
density_floor = 0.5
lane_width = 128
MESH = pl.DeviceIdType.MESH


def spread(values, slots, length):
    channels = values.shape[0]
    high_count = -(-length // lane_width)
    high_part = slots // lane_width
    low_part = slots % lane_width
    high_hot = (high_part[None, :] == jnp.arange(high_count, dtype=jnp.int32)[:, None]).astype(
        jnp.float32
    )
    low_hot = (low_part[:, None] == jnp.arange(lane_width, dtype=jnp.int32)[None, :]).astype(
        jnp.float32
    )
    left_side = (values[:, None, :] * high_hot[None]).reshape(
        channels * high_count, values.shape[1]
    )
    summed = jnp.dot(
        left_side, low_hot, precision=lax.Precision.HIGHEST, preferred_element_type=jnp.float32
    )
    return summed.reshape(channels, high_count * lane_width)


def face_value(low2, low1, high1, high2):
    return (7.0 * (low1 + high1) - (low2 + high2)) * twelfth


def gas_kernel(
    n_phi,
    n_row,
    nz,
    density,
    velocity,
    offsets,
    courants,
    mass_in,
    stop_in,
    dust_in,
    occ_in,
    move_in,
    density_out,
    velocity_out,
    kept_out,
    moved_out,
    ring_a,
    ring_b,
    swept_a,
    swept_b,
    home_a,
    home_b,
    leave,
    mass,
    stop,
    dust,
    occ,
    move,
    dust_next,
    send_sems,
    ring_sems,
    home_sems,
    rim_sems,
    rim_send_sems,
    load_sems,
):
    me = lax.axis_index("phi")
    tile = lax.axis_index("row")
    slab_rows = nz * RADIAL
    at_start = tile == 0
    at_end = tile == n_row - 1

    loads = [
        pltpu.make_async_copy(src, dst, load_sems.at[i])
        for i, (src, dst) in enumerate(
            ((mass_in, mass), (stop_in, stop), (dust_in, dust), (occ_in, occ), (move_in, move))
        )
    ]
    for load in loads:
        load.start()

    barrier = pltpu.get_barrier_semaphore()

    def greet(i, _):
        pl.semaphore_signal(
            barrier, inc=1, device_id={"phi": lax.rem(me + i, n_phi)}, device_id_type=MESH
        )
        return 0

    def greet_row(i, _):
        pl.semaphore_signal(
            barrier, inc=1, device_id={"row": lax.rem(tile + i, n_row)}, device_id_type=MESH
        )
        return 0

    lax.fori_loop(1, n_phi, greet, 0)
    lax.fori_loop(1, n_row, greet_row, 0)
    pl.semaphore_wait(barrier, n_phi + n_row - 2)

    lane = lax.broadcasted_iota(jnp.int32, (n_phi, LANES), 1)

    def to_ring(step, ring):
        def piece(source, target):
            return pltpu.make_async_remote_copy(
                src_ref=source,
                dst_ref=ring.at[pl.ds(me * RADIAL, RADIAL)],
                send_sem=send_sems.at[2 * step],
                recv_sem=ring_sems.at[step],
                device_id={"phi": target},
                device_id_type=MESH,
            )

        def own(source):
            pltpu.make_async_copy(
                source, ring.at[pl.ds(me * RADIAL, RADIAL)], ring_sems.at[step]
            ).start()

        def source_rows(ref, index):
            return ref.at[pl.ds(index * RADIAL, RADIAL)]

        if step == 0:

            def send(i, _):
                target = lax.rem(me + i, n_phi)

                @pl.when(target < nz)
                def _():
                    piece(source_rows(density, target), target).start()

                @pl.when(target >= nz)
                def _():
                    piece(source_rows(velocity, target - nz), target).start()

                return 0

            @pl.when(me < nz)
            def _():
                own(source_rows(density, me))

            @pl.when(me >= nz)
            def _():
                own(source_rows(velocity, me - nz))
        else:

            def send(i, _):
                target = lax.rem(me + i, n_phi)
                piece(source_rows(leave, target), target).start()
                return 0

            own(source_rows(leave, me))
        lax.fori_loop(1, n_phi, send, 0)
        pltpu.make_async_copy(ring, ring, ring_sems.at[step]).wait()

    def sweep(step, ring, swept):
        def one(r, _):
            x = ring[pl.ds(r, n_phi, stride=RADIAL), :]
            offset = offsets[step, r]
            hops = lax.shift_right_logical(offset, 7)
            rest = jnp.bitwise_and(offset, 127)
            x = pltpu.roll(x, hops, 0)
            x = pltpu.roll(x, rest, 1)
            x = jnp.where(lane >= rest, x, pltpu.roll(x, 1, 0))
            before = pltpu.roll(x, 1, 0)
            after = pltpu.roll(x, n_phi - 1, 0)

            def back(k):
                return pltpu.roll(jnp.where(lane < LANES - k, x, before), k, 1)

            def ahead(k):
                return pltpu.roll(jnp.where(lane >= k, x, after), LANES - k, 1)

            m1, m2, m3 = back(1), back(2), back(3)
            p1, p2, p3 = ahead(1), ahead(2), ahead(3)
            c = jnp.full((n_phi, LANES), courants[step, r], jnp.float32)
            size = jnp.abs(c)
            upwind = c >= 0.0
            f_m2 = face_value(m3, m2, m1, x)
            f_m1 = face_value(m2, m1, x, p1)
            f_0 = face_value(m1, x, p1, p2)
            f_p1 = face_value(x, p1, p2, p3)
            inner = 1.0 - size * (2.0 / 3.0)

            def flux(face, low_face, high_face, low, high):
                other = jnp.where(upwind, low_face, high_face)
                base = jnp.where(upwind, low, high)
                bend = 6.0 * base - 3.0 * (other + face)
                return face - 0.5 * size * ((face - other) - inner * bend)

            change = flux(f_0, f_m1, f_p1, x, p1) - flux(f_m1, f_m2, f_0, m1, x)
            swept[pl.ds(r, n_phi, stride=RADIAL), :] = x - c * change
            return 0

        lax.fori_loop(0, RADIAL, one, 0)

    def to_home(step, swept, home):
        base = me * SLAB + PAD

        def send(i, _):
            target = lax.rem(me + i, n_phi)
            pltpu.make_async_remote_copy(
                src_ref=swept.at[pl.ds(target * RADIAL, RADIAL)],
                dst_ref=home.at[pl.ds(base, RADIAL)],
                send_sem=send_sems.at[2 * step + 1],
                recv_sem=home_sems.at[step],
                device_id={"phi": target},
                device_id_type=MESH,
            ).start()
            return 0

        pltpu.make_async_copy(
            swept.at[pl.ds(me * RADIAL, RADIAL)], home.at[pl.ds(base, RADIAL)], home_sems.at[step]
        ).start()
        lax.fori_loop(1, n_phi, send, 0)
        pltpu.make_async_copy(swept, swept, home_sems.at[step]).wait()

    def rims(step, home):
        slabs = home.reshape(FIELDS * nz, SLAB, LANES)

        def copy(src, dst, sem, target):
            return pltpu.make_async_remote_copy(
                src_ref=slabs.at[:, pl.ds(src, 3), :],
                dst_ref=slabs.at[:, pl.ds(dst, 3), :],
                send_sem=rim_send_sems.at[2 * step + sem],
                recv_sem=rim_sems.at[2 * step + sem],
                device_id={"row": target},
                device_id_type=MESH,
            )

        up = copy(PAD + RADIAL - 3, PAD - 3, 0, tile + 1)
        down = copy(PAD, PAD + RADIAL, 1, tile - 1)

        @pl.when(jnp.logical_not(at_end))
        def _():
            up.start()

        @pl.when(jnp.logical_not(at_start))
        def _():
            down.start()

        def rows(index):
            return pl.ds(index, FIELDS * nz, stride=SLAB)

        @pl.when(at_start)
        def _():
            for j in range(3):
                home[rows(PAD - 3 + j), :] = home[rows(PAD), :]

        @pl.when(at_end)
        def _():
            for j in range(3):
                home[rows(PAD + RADIAL + j), :] = home[rows(PAD + RADIAL - 1), :]

        @pl.when(jnp.logical_not(at_end))
        def _():
            up.wait_send()
            down.wait_recv()

        @pl.when(jnp.logical_not(at_start))
        def _():
            down.wait_send()
            up.wait_recv()

    def finish(step, home):
        last = step == STEPS - 1

        def gas_row(field, index):
            return home[pl.ds(field * nz * SLAB + index, nz, stride=SLAB), :]

        def dust_rows(slot, r):
            return pl.ds(slot * slab_rows + r, nz, stride=RADIAL)

        def flux(low, high, low_face, face, high_face):
            c = radial_rate * (low[1] + high[1])
            size = jnp.abs(c)
            upwind = c >= 0.0
            inner = 1.0 - size * (2.0 / 3.0)
            half = 0.5 * size
            out = []
            for f in range(FIELDS):
                other = jnp.where(upwind, low_face[f], high_face[f])
                base = jnp.where(upwind, low[f], high[f])
                bend = 6.0 * base - 3.0 * (other + face[f])
                out.append(c * (face[f] - half * ((face[f] - other) - inner * bend)))
            return tuple(out)

        def faces(rows):
            return tuple(face_value(*(row[f] for row in rows)) for f in range(FIELDS))

        def gas_rows(index):
            return tuple(gas_row(f, index) for f in range(FIELDS))

        start = [gas_rows(PAD - 3 + j) for j in range(6)]
        face_0 = faces(start[0:4])
        face_1 = faces(start[1:5])
        face_2 = faces(start[2:6])
        first = flux(start[2], start[3], face_0, face_1, face_2)

        def one(r, carry):
            low_flux, face_low, face, cell, next1, next2 = carry
            next3 = gas_rows(r + (PAD + 3))
            face_high = faces((cell, next1, next2, next3))
            high_flux = flux(cell, next1, face_low, face, face_high)
            rho, u_r, u_p, u_z = (cell[f] - (high_flux[f] - low_flux[f]) for f in range(FIELDS))
            floored = jnp.maximum(rho, density_floor)
            live_count = occ[dust_rows(0, r), :]
            stay_count = live_count - move[dust_rows(0, r), :]
            kick_r = jnp.zeros_like(rho)
            kick_p = jnp.zeros_like(rho)
            zero = jnp.zeros_like(rho)
            kept = [zero, zero, zero]
            moved = [zero, zero, zero]
            source = dust if step == 0 else dust_next
            for k in range(K):
                live = k < live_count
                weight = mass[dust_rows(k, r), :]
                v_r = source[dust_rows(k, r), :]
                v_p = source[dust_rows(K + k, r), :]
                drag = floored * stop[dust_rows(k, r), :]
                drag = jnp.where(live, drag / (1.0 + drag), 0.0)
                d_r = drag * (u_r - v_r)
                d_p = drag * (u_p - v_p)
                kick_r = kick_r + weight * d_r
                kick_p = kick_p + weight * d_p
                v_r = v_r + d_r
                v_p = v_p + d_p
                if last:
                    stays = k < stay_count
                    stay_mass = jnp.where(stays, weight, 0.0)
                    move_mass = jnp.where(live, weight, 0.0) - stay_mass
                    for total, m in ((kept, stay_mass), (moved, move_mass)):
                        total[0] = total[0] + m
                        total[1] = total[1] + m * v_r
                        total[2] = total[2] + m * v_p
                else:
                    dust_next[dust_rows(k, r), :] = v_r
                    dust_next[dust_rows(K + k, r), :] = v_p
            scale = 1.0 / floored
            u_r = u_r - kick_r * scale
            u_p = u_p - kick_p * scale
            if last:
                density_out[dust_rows(0, r), :] = rho
                for i, value in enumerate((u_r, u_p, u_z)):
                    velocity_out[dust_rows(i, r), :] = value
                for i in range(3):
                    kept_out[dust_rows(i, r), :] = kept[i]
                    moved_out[dust_rows(i, r), :] = moved[i]
            else:
                for i, value in enumerate((rho, u_r, u_p, u_z)):
                    leave[dust_rows(i, r), :] = value
            return (high_flux, face, face_high, next1, next2, next3)

        lax.fori_loop(
            0, RADIAL, one, (first, face_1, face_2, start[3], start[4], start[5])
        )

    to_ring(0, ring_a)
    sweep(0, ring_a, swept_a)
    to_home(0, swept_a, home_a)
    rims(0, home_a)
    for load in loads:
        load.wait()
    finish(0, home_a)
    to_ring(1, ring_b)
    sweep(1, ring_b, swept_b)
    to_home(1, swept_b, home_b)
    rims(1, home_b)
    finish(1, home_b)
    partners = (n_phi - 1) * RADIAL
    for i in range(2 * STEPS):
        pltpu.make_async_copy(
            swept_a.at[pl.ds(0, partners)], swept_a.at[pl.ds(0, partners)], send_sems.at[i]
        ).wait()


def gas_and_dust(density, velocity, offsets, courants, mass, stop, dust_velocity, occ, move):
    n_phi = lax.axis_size("phi")
    n_row = lax.axis_size("row")
    nz, radial, lanes = density.shape
    cells = nz * radial

    def flat(array):
        return array.reshape(-1, lanes)

    def rows(count, dtype=jnp.float32):
        return pltpu.VMEM((count, lanes), dtype)

    def out(count):
        return jax.ShapeDtypeStruct((count * cells, lanes), jnp.float32)

    hbm = pl.BlockSpec(memory_space=pl.ANY)
    vmem = pl.BlockSpec(memory_space=pltpu.VMEM)
    smem = pl.BlockSpec(memory_space=pltpu.SMEM)
    ring = n_phi * radial
    outs = pl.pallas_call(
        functools.partial(gas_kernel, n_phi, n_row, nz),
        out_shape=(out(1), out(3), out(3), out(3)),
        in_specs=[hbm, hbm, smem, smem] + [hbm] * 5,
        out_specs=[vmem] * 4,
        scratch_shapes=[
            rows(ring),
            rows(ring),
            rows(ring),
            rows(ring),
            rows(FIELDS * nz * SLAB),
            rows(FIELDS * nz * SLAB),
            rows(FIELDS * cells),
            rows(K * cells),
            rows(K * cells),
            rows(2 * K * cells),
            rows(cells, jnp.int32),
            rows(cells, jnp.int32),
            rows(2 * K * cells),
            pltpu.SemaphoreType.DMA((2 * STEPS,)),
            pltpu.SemaphoreType.DMA((STEPS,)),
            pltpu.SemaphoreType.DMA((STEPS,)),
            pltpu.SemaphoreType.DMA((2 * STEPS,)),
            pltpu.SemaphoreType.DMA((2 * STEPS,)),
            pltpu.SemaphoreType.DMA((5,)),
        ],
        compiler_params=pltpu.CompilerParams(
            collective_id=0, has_side_effects=True, vmem_limit_bytes=32 * 1024 * 1024
        ),
    )(
        flat(density),
        flat(velocity),
        offsets,
        courants,
        flat(mass),
        flat(stop),
        flat(dust_velocity),
        flat(occ),
        flat(move),
    )
    return [value.reshape((-1, nz, radial, lanes)) for value in outs]


def body(
    gas_density,
    gas_velocity,
    orbital_offsets,
    residual_courant,
    dust_mass,
    dust_stop,
    dust_velocity,
    occupancy,
    move_count,
    dest_tile,
):
    row_devices = lax.axis_size("row")
    row_place = lax.axis_index("row")
    density, velocity, kept_grid, migrating = gas_and_dust(
        gas_density,
        gas_velocity,
        orbital_offsets,
        residual_courant,
        dust_mass,
        dust_stop,
        dust_velocity,
        occupancy,
        move_count,
    )
    tile_cells = occupancy.size
    box_slots = tile_cells // 16
    list_length = box_slots + (row_devices - 2) * (box_slots // 4)
    migrating_flat = migrating.reshape(3, tile_cells)
    dest_flat = dest_tile.reshape(tile_cells)
    moving_flat = move_count.reshape(tile_cells) > 0
    cell_numbers = jnp.arange(tile_cells, dtype=jnp.int32)
    list_rank = jnp.cumsum(moving_flat.astype(jnp.int32)) - 1
    list_slot = jnp.where(moving_flat, list_rank, list_length)
    cell_codes = (dest_flat * tile_cells + cell_numbers).astype(jnp.float32)
    code_float = spread(cell_codes[None], list_slot, list_length)[0]
    code_list = (code_float + 0.5).astype(jnp.int32)
    value_list = spread(migrating_flat, list_slot, list_length)
    all_codes, all_values = (
        lax.all_gather(code_list, "row", axis=0, tiled=True),
        lax.all_gather(value_list, "row", axis=1, tiled=True),
    )
    for_here = all_codes // tile_cells == row_place
    target_cell = jnp.where(for_here, all_codes % tile_cells, tile_cells)
    arrived = spread(all_values, target_cell, tile_cells)
    dust_grid = (kept_grid.reshape(3, tile_cells) + arrived).reshape(kept_grid.shape)
    return (density[0], velocity, dust_grid)


def solution(mesh):
    return jax.shard_map(
        body,
        mesh=mesh,
        in_specs=(
            P(None, "row", "phi"),
            P(None, None, "row", "phi"),
            P(None, "row"),
            P(None, "row"),
            P(None, None, "row", "phi"),
            P(None, None, "row", "phi"),
            P(None, None, None, "row", "phi"),
            P(None, "row", "phi"),
            P(None, "row", "phi"),
            P(None, "row", "phi"),
        ),
        out_specs=(P(None, "row", "phi"), P(None, None, "row", "phi"), P(None, None, "row", "phi")),
        check_vma=False,
    )
```

time: 277 us -> 184 us (0.66)
  waiting for transfers between devices: 118 us -> 0 us
  Pallas kernels: 0 us -> 65 us
  starting transfers between devices: 36.4 us -> 0 us
  other arithmetic: 32.6 us -> 18.8 us
  local copies, waits for them, and re-layouts: 5.64 us -> 13.8 us
  blocking collectives: 52.8 us -> 55.7 us
    ppermute x20 -> x0, waiting for transfers between devices: 118 us -> none  [the longest x12 99.9 us: shifted(): return lax.ppermute(value, axis, pairs)]
    pallas_call x0 -> x1, Pallas kernels: none -> 65 us  [gas_and_dust(): pl.pallas_call(functools.partial(gas_kernel, n_phi, n_row, nz), out_shape...]
    ppermute x20 -> x0, starting transfers between devices: 36.4 us -> none  [the longest x4 15.6 us: extended(): after = lax.ppermute(first, axis, down)]
    unnamed x16 -> x21, local copies, waits for them, and re-layouts: 0.64 us -> 9.06 us
    select_n x33 -> x0, other arithmetic: 6.48 us -> none  [the longest x14 2.86 us: shift_by_hops(): joined = jnp.where(chosen[None, None, :, None], moved, joined)]
  transfers between devices with their start and end apart: 20 -> 0, of which waited for: 16 -> 0; matrix products, arithmetic and copies ran while one was open for 5% -> 0% of each run, Pallas kernels for 0% -> 0%
where the time goes in v1:
time: 184 us; the launch traced here: 183 us
  Pallas kernels  65 us (35%)
  blocking collectives  55.7 us (30%)
  matrix products  28.9 us (16%)
  other arithmetic  18.8 us (10%)
  local copies, waits for them, and re-layouts  13.8 us (8%)
    pallas_call x1, Pallas kernels, gas_and_dust(): pl.pallas_call(functools.partial(gas_kernel, n_phi, n_row, nz), out_shape...  65 us
    dot_general x3, matrix products, spread(): jnp.dot(left_side, low_hot, precision=lax.Precision.HIGHEST, preferred_el...  28.9 us
    all_gather x1, blocking collectives, body(): lax.all_gather(value_list, 'row', axis=1, tiled=True)  28.5 us
    all_gather x1, blocking collectives, body(): lax.all_gather(code_list, 'row', axis=0, tiled=True)  27.2 us
    unnamed x21, local copies, waits for them, and re-layouts  9.06 us
    dot_general x2, other arithmetic, spread(): jnp.dot(left_side, low_hot, precision=lax.Precision.HIGHEST, preferred_el...  8.07 us
    convert_element_type x2, other arithmetic, spread(): (high_part[None, :] == jnp.arange(high_count, dtype=jnp.int32)[:, None])....  5.14 us
    mul x2, local copies, waits for them, and re-layouts, spread(): values[:, None, :] * high_hot[None]  4.29 us

profile of v1, /device:TPU:8, one launch (start us, length us, event | category | flops | bytes accessed | tf_op | source)
XLA Modules:
  0.0 182.9 jit_solution(18070900837694183831)
XLA Ops:
  0.6 0.9 broadcast_compare_fusion.1
  1.5 0.8 broadcast_multiply_fusion.1
  2.3 0.8 compare_convert_fusion.1
  3.2 0.1 copy.18
  3.3 0.2 reduce-window.9
  3.5 0.1 copy.19
  3.6 0.2 reduce-window.12
  3.8 0.1 slice_reduce_fusion
  3.9 0.1 copy.20
  4.0 0.1 add_select_fusion.5
  4.1 0.0 copy-start
  4.1 0.8 copy-done
  4.9 0.0 copy-start.1
  4.9 1.0 copy-done.1
  6.0 0.0 copy-start.2
  6.0 0.9 copy-done.2
  6.9 0.0 copy-start.3
  6.9 0.9 copy-done.3
  7.9 0.0 copy-start.4
  7.9 0.9 copy-done.4
  8.8 0.0 copy-start.5
  8.8 0.8 copy-done.5
  9.6 0.0 copy-start.6
  9.6 0.8 copy-done.6
  10.5 0.0 copy-start.7
  10.5 0.7 copy-done.7
  11.1 0.0 copy-start.8
  11.1 0.7 copy-done.8
  11.8 65.0 %shard_map.121 = (f32[128,128]{1,0:T(8,128)S(1)}, f32[384,128]{1,0:T(8,128)S(1)}, f32[384,128]{1,0:T(8,128)S(1)}, f32[384,128]{1,0:T(8,128)S(1)}) custom-call(f32[128,128]{1,0:T(8,128)S(1)} %bitcast.44, f32[384,128]{1,0:T(8,128)S(1)} %bitcast.43, s32[2,16]{1,0:T(2,128)S(1)} %copy-done.7, f32[2,16]{1,0:T(2,128)S(1)} %copy-done.8, f32[512,128]{1,0:T(8,128)S(1)} %bitcast.39, ...), custom_call_target="tpu_custom_call" | custom-call | tf_op jit(solution)/shard_map/pallas_call | solution.py:413
  76.8 0.1 mul.58
  76.9 0.1 fusion.47
  77.0 3.4 %fusion.21 = s32[20,128]{1,0:T(8,128)S(1)} fusion(s32[16384]{0:T(1024)S(1)} %get-tuple-element.14, f32[20,16384]{1,0:T(8,128)S(1)} %fusion.47), kind=kOutput, calls=%fused_computation.19 | convolution fusion | flops 505418752 | bytes 1386496 | tf_op jit(solution)/shard_map/dot_general | solution.py:39
  80.5 27.2 %all-gather = s32[8,1,2560]{2,1,0:T(1,128)S(1)} all-gather(s32[1,1,2560]{2,1,0:T(1,128)S(1)} %reshape.239), channel_id=1, replica_groups=mesh['phi'=32,'row'=8] {'row'}, dimensions={0}, use_global_device_ids=true | all-gather | bytes 92160 | tf_op jit(solution)/shard_map/all_gather | solution.py:495
  107.7 0.1 add_select_fusion.1
  107.8 0.1 fusion.12
  108.0 2.5 %broadcast_multiply_fusion = f32[3,20,16384]{2,1,0:T(8,128)} fusion(f32[20,16384]{1,0:T(8,128)S(1)} %fusion.12, f32[3,16384]{1,0:T(4,128)S(1)} %mul.58), kind=kLoop, calls=%fused_computation.13 | loop fusion | flops 983040 | bytes 5439488 | tf_op jit(solution)/shard_map/mul | solution.py:36
  110.5 4.2 %mul.62 = f32[60,16384]{1,0:T(8,128)} reshape(f32[3,20,16384]{2,1,0:T(8,128)} %broadcast_multiply_fusion) | data formatting | bytes 7864320 | tf_op jit(solution)/shard_map/mul | solution.py:36
  114.6 5.7 %fusion.7 = f32[60,128]{1,0:T(8,128)S(1)} fusion(f32[60,16384]{1,0:T(8,128)} %mul.62, s32[16384]{0:T(1024)S(1)} %get-tuple-element.14), kind=kOutput, calls=%fused_computation.9 | convolution fusion | flops 1512046592 | bytes 4028416 | tf_op jit(solution)/shard_map/dot_general | solution.py:39
  120.4 28.5 %all_gather.6 = f32[3,20480]{1,0:T(4,128)S(1)} all-gather(f32[3,2560]{1,0:T(4,128)S(1)} %reshape.238), channel_id=1, replica_groups=mesh['phi'=32,'row'=8] {'row'}, dimensions={1}, use_global_device_ids=true | all-gather | bytes 276480 | tf_op jit(solution)/shard_map/all_gather | solution.py:496
  148.9 5.0 %compare_convert_fusion = f32[8,16,20480]{2,1,0:T(8,128)} fusion(s32[8,16]{1,0:T(8,128)S(1)} %multiply_add_fusion, s32[20480]{0:T(1024)S(1)} %get-tuple-element.11), kind=kLoop, calls=%fused_computation.6 | loop fusion | flops 5242880 | bytes 10568192 | tf_op jit(solution)/shard_map/convert_element_type | solution.py:30
  153.9 7.9 %fusion.45 = f32[3,8,16,20480]{3,2,1,0:T(8,128)S(1)} fusion(f32[8,16,20480]{2,1,0:T(8,128)} %compare_convert_fusion, f32[3,20480]{1,0:T(4,128)S(1)} %all_gather.6), kind=kLoop, calls=%fused_computation.1.clone.clone.clone.2 | loop fusion | flops 7864320 | bytes 42188800 | tf_op jit(solution)/shard_map/dot_general | solution.py:39
  161.9 19.7 %fusion.13 = f32[3,8,16,128]{3,2,1,0:T(8,128)} fusion(f32[3,8,16,128]{3,2,1,0:T(8,128)S(1)} %bitcast.41, s32[20480]{0:T(1024)S(1)} %get-tuple-element.12, f32[3,8,16,20480]{3,2,1,0:T(8,128)S(1)} %fusion.45), kind=kOutput, calls=%fused_computation.17 | convolution fusion | flops 12082266112 | bytes 31932416 | tf_op jit(solution)/shard_map/dot_general | solution.py:39
  181.6 0.6 copy.24
  182.2 0.7 copy.25
  (5 shorter events, 0.1 us)
Async XLA Ops:
  4.1 0.8 copy-start
  4.9 1.0 copy-start.1
  6.0 0.9 copy-start.2
  6.9 0.9 copy-start.3
  7.9 0.9 copy-start.4
  8.8 0.8 copy-start.5
  9.6 0.8 copy-start.6
  10.5 0.7 copy-start.7
  11.1 0.7 copy-start.8

commit v2 on v1

--- a/solution.py
+++ b/solution.py
@@ -18,32 +18,106 @@
 twelfth = 1.0 / 12.0
 radial_rate = 0.15
 density_floor = 0.5
-lane_width = 128
+LIST = 24
+DEST_BIT = 14
+HAS_BIT = 17
+BITS = 14
 MESH = pl.DeviceIdType.MESH
-
-
-def spread(values, slots, length):
-    channels = values.shape[0]
-    high_count = -(-length // lane_width)
-    high_part = slots // lane_width
-    low_part = slots % lane_width
-    high_hot = (high_part[None, :] == jnp.arange(high_count, dtype=jnp.int32)[:, None]).astype(
-        jnp.float32
-    )
-    low_hot = (low_part[:, None] == jnp.arange(lane_width, dtype=jnp.int32)[None, :]).astype(
-        jnp.float32
-    )
-    left_side = (values[:, None, :] * high_hot[None]).reshape(
-        channels * high_count, values.shape[1]
-    )
-    summed = jnp.dot(
-        left_side, low_hot, precision=lax.Precision.HIGHEST, preferred_element_type=jnp.float32
-    )
-    return summed.reshape(channels, high_count * lane_width)
 
 
 def face_value(low2, low1, high1, high2):
     return (7.0 * (low1 + high1) - (low2 + high2)) * twelfth
+
+
+def indices(shape):
+    return (
+        lax.broadcasted_iota(jnp.int32, shape, 1),
+        lax.broadcasted_iota(jnp.int32, shape, 2),
+    )
+
+
+def later(x, count):
+    return jnp.concatenate([x[count:], jnp.zeros_like(x[:count])], axis=0)
+
+
+def earlier(x, count):
+    return jnp.concatenate([jnp.zeros_like(x[:count]), x[:-count]], axis=0)
+
+
+def moved_down(x, bit):
+    sub, lane = indices(x.shape)
+    if bit >= 10:
+        return later(x, 1 << (bit - 10))
+    if bit >= 3:
+        step = 1 << (bit - 3)
+        return pltpu.roll(jnp.where(lane < step, later(x, 1), x), LANES - step, 2)
+    step = 1 << bit
+    turned = pltpu.roll(x, 8 - step, 1)
+    carried = pltpu.roll(jnp.where(lane == 0, later(turned, 1), turned), LANES - 1, 2)
+    return jnp.where(sub < 8 - step, turned, carried)
+
+
+def moved_up(x, bit):
+    sub, lane = indices(x.shape)
+    if bit >= 10:
+        return earlier(x, 1 << (bit - 10))
+    if bit >= 3:
+        step = 1 << (bit - 3)
+        return pltpu.roll(jnp.where(lane >= LANES - step, earlier(x, 1), x), step, 2)
+    step = 1 << bit
+    turned = pltpu.roll(x, step, 1)
+    carried = pltpu.roll(jnp.where(lane == LANES - 1, earlier(turned, 1), turned), 1, 2)
+    return jnp.where(sub >= step, turned, carried)
+
+
+def has_bit(word, bit):
+    return jnp.bitwise_and(word, 1 << bit) != 0
+
+
+def compact(values, picks):
+    for bit in range(BITS):
+        chosen = has_bit(picks, bit)
+        values = [jnp.where(chosen, moved_down(x, bit), x) for x in values]
+    return [x[: LIST // 8] for x in values]
+
+
+def expand(lists, route, blocks):
+    values = [
+        jnp.concatenate([x, jnp.zeros((blocks - LIST // 8, 8, LANES), x.dtype)], axis=0)
+        for x in lists
+    ]
+    for bit in reversed(range(BITS)):
+        chosen = has_bit(route, bit)
+        values = [jnp.where(chosen, moved_up(x, bit), x) for x in values]
+    return values
+
+
+def move_plan(has):
+    sub, lane = indices(has.shape)
+    empty = jnp.where(has, 0, 1)
+    ahead = empty
+    for step in (1, 2, 4):
+        ahead = ahead + jnp.where(sub >= step, pltpu.roll(ahead, step, 1), 0)
+    column = jnp.broadcast_to(ahead[:, 7:8, :], has.shape)
+    across = column
+    for step in (1, 2, 4, 8, 16, 32, 64):
+        across = across + jnp.where(lane >= step, pltpu.roll(across, step, 2), 0)
+    whole = jnp.broadcast_to(across[:, :, LANES - 1 :], has.shape)
+    sums = [jnp.zeros_like(whole[0])]
+    for block in range(has.shape[0] - 1):
+        sums.append(sums[-1] + whole[block])
+    distance = ahead - empty + across - column + jnp.stack(sums)
+    way = jnp.where(has, distance, 0)
+    starts = jnp.zeros_like(way)
+    ends = jnp.zeros_like(way)
+    for bit in range(BITS):
+        here = jnp.bitwise_and(way, 1 << bit)
+        starts = jnp.bitwise_or(starts, here)
+        coming = moved_down(way, bit)
+        arriving = jnp.bitwise_and(coming, 1 << bit)
+        ends = jnp.bitwise_or(ends, arriving)
+        way = jnp.where(arriving != 0, coming, jnp.where(here != 0, 0, way))
+    return starts, ends
 
 
 def gas_kernel(
@@ -59,10 +133,10 @@
     dust_in,
     occ_in,
     move_in,
+    dest_in,
     density_out,
     velocity_out,
-    kept_out,
-    moved_out,
+    dust_out,
     ring_a,
     ring_b,
     swept_a,
@@ -75,12 +149,24 @@
     dust,
     occ,
     move,
+    dest,
     dust_next,
+    picks,
+    route,
+    routes,
+    mass_list,
+    mass_lists,
+    push_list,
+    push_lists,
+    moved,
+    grid,
     send_sems,
     ring_sems,
     home_sems,
     rim_sems,
     rim_send_sems,
+    list_send_sems,
+    list_sems,
     load_sems,
 ):
     me = lax.axis_index("phi")
@@ -92,7 +178,7 @@
     loads = [
         pltpu.make_async_copy(src, dst, load_sems.at[i])
         for i, (src, dst) in enumerate(
-            ((mass_in, mass), (stop_in, stop), (dust_in, dust), (occ_in, occ), (move_in, move))
+            ((mass_in, mass), (stop_in, stop), (dust_in, dust), (occ_in, occ), (move_in, move), (dest_in, dest))
         )
     ]
     for load in loads:
@@ -117,6 +203,11 @@
     pl.semaphore_wait(barrier, n_phi + n_row - 2)
 
     lane = lax.broadcasted_iota(jnp.int32, (n_phi, LANES), 1)
+
+    def far_first(i):
+        half = lax.shift_right_logical(i, 1)
+        ahead = jnp.where(jnp.bitwise_and(i, 1) == 1, n_phi // 2 + half, n_phi // 2 - half)
+        return lax.rem(me + ahead, n_phi)
 
     def to_ring(step, ring):
         def piece(source, target):
@@ -140,7 +231,7 @@
         if step == 0:
 
             def send(i, _):
-                target = lax.rem(me + i, n_phi)
+                target = far_first(i)
 
                 @pl.when(target < nz)
                 def _():
@@ -162,12 +253,14 @@
         else:
 
             def send(i, _):
-                target = lax.rem(me + i, n_phi)
+                target = far_first(i)
                 piece(source_rows(leave, target), target).start()
                 return 0
 
             own(source_rows(leave, me))
         lax.fori_loop(1, n_phi, send, 0)
+
+    def ring_wait(step, ring):
         pltpu.make_async_copy(ring, ring, ring_sems.at[step]).wait()
 
     def sweep(step, ring, swept):
@@ -215,7 +308,7 @@
         base = me * SLAB + PAD
 
         def send(i, _):
-            target = lax.rem(me + i, n_phi)
+            target = far_first(i)
             pltpu.make_async_remote_copy(
                 src_ref=swept.at[pl.ds(target * RADIAL, RADIAL)],
                 dst_ref=home.at[pl.ds(base, RADIAL)],
@@ -323,11 +416,12 @@
             floored = jnp.maximum(rho, density_floor)
             live_count = occ[dust_rows(0, r), :]
             stay_count = live_count - move[dust_rows(0, r), :]
+            spot = pl.ds(pl.multiple_of(r * nz, nz), nz)
             kick_r = jnp.zeros_like(rho)
             kick_p = jnp.zeros_like(rho)
             zero = jnp.zeros_like(rho)
-            kept = [zero, zero, zero]
-            moved = [zero, zero, zero]
+            kept_push = [zero, zero]
+            moved_push = [zero, zero]
             source = dust if step == 0 else dust_next
             for k in range(K):
                 live = k < live_count
@@ -346,10 +440,9 @@
                     stays = k < stay_count
                     stay_mass = jnp.where(stays, weight, 0.0)
                     move_mass = jnp.where(live, weight, 0.0) - stay_mass
-                    for total, m in ((kept, stay_mass), (moved, move_mass)):
-                        total[0] = total[0] + m
-                        total[1] = total[1] + m * v_r
-                        total[2] = total[2] + m * v_p
+                    for total, m in ((kept_push, stay_mass), (moved_push, move_mass)):
+                        total[0] = total[0] + m * v_r
+                        total[1] = total[1] + m * v_p
                 else:
                     dust_next[dust_rows(k, r), :] = v_r
                     dust_next[dust_rows(K + k, r), :] = v_p
@@ -360,9 +453,9 @@
                 density_out[dust_rows(0, r), :] = rho
                 for i, value in enumerate((u_r, u_p, u_z)):
                     velocity_out[dust_rows(i, r), :] = value
-                for i in range(3):
-                    kept_out[dust_rows(i, r), :] = kept[i]
-                    moved_out[dust_rows(i, r), :] = moved[i]
+                for i in range(2):
+                    grid[i + 1, spot, :] = kept_push[i]
+                    moved[i, spot, :] = moved_push[i]
             else:
                 for i, value in enumerate((rho, u_r, u_p, u_z)):
                     leave[dust_rows(i, r), :] = value
@@ -372,18 +465,116 @@
             0, RADIAL, one, (first, face_1, face_2, start[3], start[4], start[5])
         )
 
+    def blocks(value):
+        return value.reshape(RADIAL, nz, LANES)
+
+    def plan():
+        def one(r, _):
+            rows = pl.ds(r, nz, stride=RADIAL)
+            spot = pl.ds(pl.multiple_of(r * nz, nz), nz)
+            live_count = occ[rows, :]
+            leaving = move[rows, :]
+            stay_count = live_count - leaving
+            kept_mass = jnp.zeros((nz, LANES), jnp.float32)
+            moved_mass = jnp.zeros((nz, LANES), jnp.float32)
+            for k in range(K):
+                weight = mass[pl.ds(k * slab_rows + r, nz, stride=RADIAL), :]
+                stays = k < stay_count
+                kept_mass = kept_mass + jnp.where(stays, weight, 0.0)
+                goes = jnp.logical_and(k < live_count, jnp.logical_not(stays))
+                moved_mass = moved_mass + jnp.where(goes, weight, 0.0)
+            grid[0, spot, :] = kept_mass
+            moved[0, spot, :] = moved_mass
+            picks[spot, :] = leaving
+            route[spot, :] = dest[rows, :]
+            return 0
+
+        lax.fori_loop(0, RADIAL, one, 0)
+        has = blocks(picks[...]) > 0
+        goal = blocks(route[...])
+        starts, ends = move_plan(has)
+        picks[...] = ends.reshape(slab_rows, LANES)
+        marks = jnp.where(has, 1 << HAS_BIT, 0) + goal * (1 << DEST_BIT)
+        route[...] = jnp.bitwise_or(starts, marks).reshape(slab_rows, LANES)
+        (listed,) = compact([blocks(moved[0])], ends)
+        mass_list[...] = listed.reshape(LIST, LANES)
+
+    def to_tiles(pairs):
+        def send(i, _):
+            target = lax.rem(tile + i, n_row)
+            for number, source, landing in pairs:
+                count = source.shape[0]
+                pltpu.make_async_remote_copy(
+                    src_ref=source,
+                    dst_ref=landing.at[pl.ds(tile * count, count)],
+                    send_sem=list_send_sems.at[number],
+                    recv_sem=list_sems.at[number],
+                    device_id={"row": target},
+                    device_id_type=MESH,
+                ).start()
+            return 0
+
+        lax.fori_loop(1, n_row, send, 0)
+
+    def tiles_wait(pairs, sems):
+        for number, source, landing in pairs:
+            part = landing.at[pl.ds(0, (n_row - 1) * source.shape[0])]
+            pltpu.make_async_copy(part, part, sems.at[number]).wait()
+
+    def gather(number, landing, count):
+        def one(i, _):
+            source = lax.rem(tile + i, n_row)
+            code = blocks(routes[pl.ds(source * slab_rows, slab_rows), :])
+            lists = [
+                landing[pl.ds((source * count + j) * LIST, LIST), :].reshape(LIST // 8, 8, LANES)
+                for j in range(count)
+            ]
+            spread = expand(lists, code, RADIAL)
+            wanted = lax.shift_right_logical(code, DEST_BIT) == tile + (1 << (HAS_BIT - DEST_BIT))
+            for j in range(count):
+                added = jnp.where(wanted, spread[j], 0.0).reshape(slab_rows, LANES)
+                grid[number + j] = grid[number + j] + added
+            return 0
+
+        lax.fori_loop(1, n_row, one, 0)
+
+    early = ((0, route, routes), (1, mass_list, mass_lists))
+    late = ((2, push_list, push_lists),)
+
     to_ring(0, ring_a)
+    for load in loads:
+        load.wait()
+    plan()
+    to_tiles(early)
+    ring_wait(0, ring_a)
     sweep(0, ring_a, swept_a)
     to_home(0, swept_a, home_a)
     rims(0, home_a)
-    for load in loads:
-        load.wait()
     finish(0, home_a)
     to_ring(1, ring_b)
+    tiles_wait(early, list_sems)
+    gather(0, mass_lists, 1)
+    ring_wait(1, ring_b)
     sweep(1, ring_b, swept_b)
     to_home(1, swept_b, home_b)
     rims(1, home_b)
     finish(1, home_b)
+    pushes = compact([blocks(moved[0]), blocks(moved[1])], blocks(picks[...]))
+    push_list[pl.ds(0, LIST), :] = pushes[0].reshape(LIST, LANES)
+    push_list[pl.ds(LIST, LIST), :] = pushes[1].reshape(LIST, LANES)
+    to_tiles(late)
+    tiles_wait(late, list_sems)
+    gather(1, push_lists, 2)
+
+    def write(r, _):
+        spot = pl.ds(pl.multiple_of(r * nz, nz), nz)
+        for i in range(3):
+            dust_out[pl.ds(i * slab_rows + r, nz, stride=RADIAL), :] = grid[i, spot, :]
+        return 0
+
+    lax.fori_loop(0, RADIAL, write, 0)
+    tiles_wait(early, list_send_sems)
+    tiles_wait(late, list_send_sems)
     partners = (n_phi - 1) * RADIAL
     for i in range(2 * STEPS):
         pltpu.make_async_copy(
@@ -391,7 +582,7 @@
         ).wait()
 
 
-def gas_and_dust(density, velocity, offsets, courants, mass, stop, dust_velocity, occ, move):
+def gas_and_dust(density, velocity, offsets, courants, mass, stop, dust_velocity, occ, move, dest):
     n_phi = lax.axis_size("phi")
     n_row = lax.axis_size("row")
     nz, radial, lanes = density.shape
@@ -412,9 +603,9 @@
     ring = n_phi * radial
     outs = pl.pallas_call(
         functools.partial(gas_kernel, n_phi, n_row, nz),
-        out_shape=(out(1), out(3), out(3), out(3)),
-        in_specs=[hbm, hbm, smem, smem] + [hbm] * 5,
-        out_specs=[vmem] * 4,
+        out_shape=(out(1), out(3), out(3)),
+        in_specs=[hbm, hbm, smem, smem] + [hbm] * 6,
+        out_specs=[vmem] * 3,
         scratch_shapes=[
             rows(ring),
             rows(ring),
@@ -428,16 +619,28 @@
             rows(2 * K * cells),
             rows(cells, jnp.int32),
             rows(cells, jnp.int32),
+            rows(cells, jnp.int32),
             rows(2 * K * cells),
+            rows(cells, jnp.int32),
+            rows(cells, jnp.int32),
+            rows(n_row * cells, jnp.int32),
+            rows(LIST),
+            rows(n_row * LIST),
+            rows(2 * LIST),
+            rows(2 * n_row * LIST),
+            pltpu.VMEM((2, cells, lanes), jnp.float32),
+            pltpu.VMEM((3, cells, lanes), jnp.float32),
             pltpu.SemaphoreType.DMA((2 * STEPS,)),
             pltpu.SemaphoreType.DMA((STEPS,)),
             pltpu.SemaphoreType.DMA((STEPS,)),
             pltpu.SemaphoreType.DMA((2 * STEPS,)),
             pltpu.SemaphoreType.DMA((2 * STEPS,)),
-            pltpu.SemaphoreType.DMA((5,)),
+            pltpu.SemaphoreType.DMA((3,)),
+            pltpu.SemaphoreType.DMA((3,)),
+            pltpu.SemaphoreType.DMA((6,)),
         ],
         compiler_params=pltpu.CompilerParams(
-            collective_id=0, has_side_effects=True, vmem_limit_bytes=32 * 1024 * 1024
+            collective_id=0, has_side_effects=True, vmem_limit_bytes=56 * 1024 * 1024
         ),
     )(
         flat(density),
@@ -449,6 +652,7 @@
         flat(dust_velocity),
         flat(occ),
         flat(move),
+        flat(dest),
     )
     return [value.reshape((-1, nz, radial, lanes)) for value in outs]
 
@@ -465,9 +669,7 @@
     move_count,
     dest_tile,
 ):
-    row_devices = lax.axis_size("row")
-    row_place = lax.axis_index("row")
-    density, velocity, kept_grid, migrating = gas_and_dust(
+    density, velocity, dust_grid = gas_and_dust(
         gas_density,
         gas_velocity,
         orbital_offsets,
@@ -477,28 +679,8 @@
         dust_velocity,
         occupancy,
         move_count,
+        dest_tile,
     )
-    tile_cells = occupancy.size
-    box_slots = tile_cells // 16
-    list_length = box_slots + (row_devices - 2) * (box_slots // 4)
-    migrating_flat = migrating.reshape(3, tile_cells)
-    dest_flat = dest_tile.reshape(tile_cells)
-    moving_flat = move_count.reshape(tile_cells) > 0
-    cell_numbers = jnp.arange(tile_cells, dtype=jnp.int32)
-    list_rank = jnp.cumsum(moving_flat.astype(jnp.int32)) - 1
-    list_slot = jnp.where(moving_flat, list_rank, list_length)
-    cell_codes = (dest_flat * tile_cells + cell_numbers).astype(jnp.float32)
-    code_float = spread(cell_codes[None], list_slot, list_length)[0]
-    code_list = (code_float + 0.5).astype(jnp.int32)
-    value_list = spread(migrating_flat, list_slot, list_length)
-    all_codes, all_values = (
-        lax.all_gather(code_list, "row", axis=0, tiled=True),
-        lax.all_gather(value_list, "row", axis=1, tiled=True),
-    )
-    for_here = all_codes // tile_cells == row_place
-    target_cell = jnp.where(for_here, all_codes % tile_cells, tile_cells)
-    arrived = spread(all_values, target_cell, tile_cells)
-    dust_grid = (kept_grid.reshape(3, tile_cells) + arrived).reshape(kept_grid.shape)
     return (density[0], velocity, dust_grid)
 
 

time: 184 us -> 82.3 us (0.45)
  blocking collectives: 55.7 us -> 0 us
  matrix products: 28.9 us -> 0 us
  other arithmetic: 18.8 us -> 0 us
  Pallas kernels: 65 us -> 77.7 us
  local copies, waits for them, and re-layouts: 13.8 us -> 3.81 us
    all_gather x2 -> x0, blocking collectives: 55.7 us -> none  [the longest x1 28.5 us: body(): lax.all_gather(value_list, 'row', axis=1, tiled=True)]
    dot_general x3 -> x0, matrix products: 28.9 us -> none  [spread(): jnp.dot(left_side, low_hot, precision=lax.Precision.HIGHEST, preferred_el...]
    pallas_call x1, Pallas kernels: 65 us -> 77.7 us  [gas_and_dust(): pl.pallas_call(functools.partial(gas_kernel, n_phi, n_row, nz), out_shape...]
    dot_general x2 -> x0, other arithmetic: 8.07 us -> none  [spread(): jnp.dot(left_side, low_hot, precision=lax.Precision.HIGHEST, preferred_el...]
    convert_element_type x3 -> x0, other arithmetic: 5.99 us -> none  [the longest x2 5.14 us: spread(): (high_part[None, :] == jnp.arange(high_count, dtype=jnp.int32)[:, None])....]
    unnamed x21 -> x5, local copies, waits for them, and re-layouts: 9.06 us -> 3.81 us
    mul x2 -> x0, local copies, waits for them, and re-layouts: 4.29 us -> none  [spread(): values[:, None, :] * high_hot[None]]
    mul x2 -> x0, other arithmetic: 3.34 us -> none  [the longest x1 2.5 us: spread(): values[:, None, :] * high_hot[None]]
where the time goes in v2:
time: 82.3 us; the launch traced here: 82.2 us
  Pallas kernels  77.7 us (94%)
  local copies, waits for them, and re-layouts  3.81 us (5%)
    pallas_call x1, Pallas kernels, gas_and_dust(): pl.pallas_call(functools.partial(gas_kernel, n_phi, n_row, nz), out_shape...  77.7 us
    unnamed x5, local copies, waits for them, and re-layouts  3.81 us

profile of v2, /device:TPU:8, one launch (start us, length us, event | category | flops | bytes accessed | tf_op | source)
XLA Modules:
  0.0 82.2 jit_solution(11380937717297287582)
XLA Ops:
  0.6 77.7 %shard_map.121 = (f32[128,128]{1,0:T(8,128)}, f32[384,128]{1,0:T(8,128)}, f32[384,128]{1,0:T(8,128)}) custom-call(f32[128,128]{1,0:T(8,128)} %bitcast.17, f32[384,128]{1,0:T(8,128)} %bitcast.16, s32[2,16]{1,0:T(2,128)} %offsets.1, f32[2,16]{1,0:T(2,128)} %courants.1, f32[512,128]{1,0:T(8,128)} %bitcast.12, f32[512,128]{1,0:T(8,128)} %bitcast.13, ...), custom_call_target="tpu_custom_call" | custom-call | tf_op jit(solution)/shard_map/pallas_call | solution.py:604
  78.4 1.5 %copy.16 = f32[8,16,128]{2,1,0:T(8,128)} copy(f32[8,16,128]{2,1,0:T(8,128)} %bitcast.21) | data formatting | bytes 131072
  79.8 0.0 copy-start
  79.8 1.7 %copy.17 = f32[3,8,16,128]{3,2,1,0:T(8,128)} copy(f32[3,8,16,128]{3,2,1,0:T(8,128)} %bitcast.15) | data formatting | bytes 393216
  81.5 0.0 copy-done
  81.5 0.7 copy.18
Async XLA Ops:
  79.8 1.7 %copy-start = (f32[384,128]{1,0:T(8,128)S(1)}, f32[384,128]{1,0:T(8,128)}, u32[]{:S(2)}) copy-start(f32[384,128]{1,0:T(8,128)} %get-tuple-element.8) | copy-start | bytes 589828

commit v3 on v2

v3 whole, which is shorter than its diff:
```python
import functools

import jax
import jax.numpy as jnp
from jax import lax
from jax.experimental import pallas as pl
from jax.experimental.pallas import tpu as pltpu
from jax.sharding import PartitionSpec as P

K = 4
STEPS = 2
FIELDS = 4
RADIAL = 16
LANES = 128
PAD = 8
SLAB = RADIAL + 2 * PAD

twelfth = 1.0 / 12.0
radial_rate = 0.15
density_floor = 0.5
LIST = 24
DEST_BIT = 14
HAS_BIT = 17
BITS = 14
CHUNKS = 4
MESH = pl.DeviceIdType.MESH


def face_value(low2, low1, high1, high2):
    return (7.0 * (low1 + high1) - (low2 + high2)) * twelfth


def indices(shape):
    return (
        lax.broadcasted_iota(jnp.int32, shape, 1),
        lax.broadcasted_iota(jnp.int32, shape, 2),
    )


def later(x, count):
    return jnp.concatenate([x[count:], jnp.zeros_like(x[:count])], axis=0)


def earlier(x, count):
    return jnp.concatenate([jnp.zeros_like(x[:count]), x[:-count]], axis=0)


def moved_down(x, bit):
    sub, lane = indices(x.shape)
    if bit >= 10:
        return later(x, 1 << (bit - 10))
    if bit >= 3:
        step = 1 << (bit - 3)
        return pltpu.roll(jnp.where(lane < step, later(x, 1), x), LANES - step, 2)
    step = 1 << bit
    turned = pltpu.roll(x, 8 - step, 1)
    carried = pltpu.roll(jnp.where(lane == 0, later(turned, 1), turned), LANES - 1, 2)
    return jnp.where(sub < 8 - step, turned, carried)


def moved_up(x, bit):
    sub, lane = indices(x.shape)
    if bit >= 10:
        return earlier(x, 1 << (bit - 10))
    if bit >= 3:
        step = 1 << (bit - 3)
        return pltpu.roll(jnp.where(lane >= LANES - step, earlier(x, 1), x), step, 2)
    step = 1 << bit
    turned = pltpu.roll(x, step, 1)
    carried = pltpu.roll(jnp.where(lane == LANES - 1, earlier(turned, 1), turned), 1, 2)
    return jnp.where(sub >= step, turned, carried)


def has_bit(word, bit):
    return jnp.bitwise_and(word, 1 << bit) != 0


def compact(values, picks):
    for bit in range(BITS):
        chosen = has_bit(picks, bit)
        values = [jnp.where(chosen, moved_down(x, bit), x) for x in values]
    return [x[: LIST // 8] for x in values]


def expand(lists, route, blocks):
    values = [
        jnp.concatenate([x, jnp.zeros((blocks - LIST // 8, 8, LANES), x.dtype)], axis=0)
        for x in lists
    ]
    for bit in reversed(range(BITS)):
        chosen = has_bit(route, bit)
        values = [jnp.where(chosen, moved_up(x, bit), x) for x in values]
    return values


def move_plan(has):
    sub, lane = indices(has.shape)
    empty = jnp.where(has, 0, 1)
    ahead = empty
    for step in (1, 2, 4):
        ahead = ahead + jnp.where(sub >= step, pltpu.roll(ahead, step, 1), 0)
    column = jnp.broadcast_to(ahead[:, 7:8, :], has.shape)
    across = column
    for step in (1, 2, 4, 8, 16, 32, 64):
        across = across + jnp.where(lane >= step, pltpu.roll(across, step, 2), 0)
    whole = jnp.broadcast_to(across[:, :, LANES - 1 :], has.shape)
    sums = [jnp.zeros_like(whole[0])]
    for block in range(has.shape[0] - 1):
        sums.append(sums[-1] + whole[block])
    distance = ahead - empty + across - column + jnp.stack(sums)
    way = jnp.where(has, distance, 0)
    starts = jnp.zeros_like(way)
    ends = jnp.zeros_like(way)
    for bit in range(BITS):
        here = jnp.bitwise_and(way, 1 << bit)
        starts = jnp.bitwise_or(starts, here)
        coming = moved_down(way, bit)
        arriving = jnp.bitwise_and(coming, 1 << bit)
        ends = jnp.bitwise_or(ends, arriving)
        way = jnp.where(arriving != 0, coming, jnp.where(here != 0, 0, way))
    return starts, ends


def gas_kernel(
    n_phi,
    n_row,
    nz,
    density,
    velocity,
    offsets,
    courants,
    mass_in,
    stop_in,
    dust_in,
    occ_in,
    move_in,
    dest_in,
    gas_out,
    dust_out,
    ring_a,
    ring_b,
    swept_a,
    swept_b,
    home_a,
    home_b,
    leave,
    final,
    mass,
    stop,
    dust,
    occ,
    move,
    dest,
    live_mass,
    stay_mass,
    slot_stop,
    slot_radial,
    slot_azimuth,
    picks,
    route,
    routes,
    mass_list,
    mass_lists,
    push_list,
    push_lists,
    leaving_mass,
    push,
    grid,
    send_sems,
    ring_sems,
    home_sems,
    rim_sems,
    rim_send_sems,
    list_send_sems,
    list_sems,
    load_sems,
    store_sems,
):
    me = lax.axis_index("phi")
    tile = lax.axis_index("row")
    slab_rows = nz * RADIAL
    at_start = tile == 0
    at_end = tile == n_row - 1
    my_chip = lax.shift_right_logical(me, 2)
    my_side = jnp.bitwise_and(lax.shift_right_logical(me, 1), 1)
    my_core = jnp.bitwise_and(me, 1)
    my_chunk = 2 * jnp.bitwise_and(my_chip, 1) + my_core
    my_field = lax.shift_right_logical(my_chip, 1)
    my_slab = 8 * my_chunk + 4 * my_side + my_field

    loads = [
        pltpu.make_async_copy(src, dst, load_sems.at[i])
        for i, (src, dst) in enumerate(
            (
                (mass_in, mass),
                (stop_in, stop),
                (dust_in, dust),
                (occ_in, occ),
                (move_in, move),
                (dest_in, dest),
            )
        )
    ]

    barrier = pltpu.get_barrier_semaphore()

    def greet(i, _):
        pl.semaphore_signal(
            barrier, inc=1, device_id={"phi": lax.rem(me + i, n_phi)}, device_id_type=MESH
        )
        return 0

    def greet_row(i, _):
        pl.semaphore_signal(
            barrier, inc=1, device_id={"row": lax.rem(tile + i, n_row)}, device_id_type=MESH
        )
        return 0

    lax.fori_loop(1, n_phi, greet, 0)
    lax.fori_loop(1, n_row, greet_row, 0)
    for load in loads:
        load.start()
    pl.semaphore_wait(barrier, n_phi + n_row - 2)

    lane = lax.broadcasted_iota(jnp.int32, (n_phi, LANES), 1)
    sub = lax.broadcasted_iota(jnp.int32, (8, LANES), 0)
    part = jnp.bitwise_and(sub, 3)
    even = jnp.bitwise_and(sub, 1) == 0

    def far_first(i):
        half = lax.shift_right_logical(i, 1)
        ahead = jnp.where(jnp.bitwise_and(i, 1) == 1, n_phi // 2 + half, n_phi // 2 - half)
        return lax.rem(me + ahead, n_phi)

    def to_ring(step, chunk, ring):
        landing = ring.at[pl.ds(me * RADIAL, RADIAL)]

        def go(source, target):
            pltpu.make_async_remote_copy(
                src_ref=source,
                dst_ref=landing,
                send_sem=send_sems.at[2 * step],
                recv_sem=ring_sems.at[step],
                device_id={"phi": target},
                device_id_type=MESH,
            ).start()

        def stay(source):
            pltpu.make_async_copy(source, landing, ring_sems.at[step]).start()

        def place(j):
            pair = lax.shift_right_logical(j, 1)
            turn = jnp.bitwise_xor(2, jnp.bitwise_xor(pair, lax.shift_right_logical(pair, 1)))
            field = jnp.bitwise_xor(my_field, turn)
            side = jnp.bitwise_xor(my_side, jnp.bitwise_xor(jnp.bitwise_and(j, 1), 1))
            target = (2 * field + chunk // 2) * 4 + 2 * side + chunk % 2
            return field, 2 * chunk + side, target

        def rows(ref, index):
            return ref.at[pl.ds(index * RADIAL, RADIAL)]

        def each(field, height, act):
            if step == 0:

                @pl.when(field == 0)
                def _():
                    act(rows(density, height))

                @pl.when(field > 0)
                def _():
                    act(rows(velocity, (field - 1) * nz + height))
            else:
                act(rows(leave, height * FIELDS + field))

        def send(j, _):
            field, height, target = place(j)
            each(field, height, lambda source: go(source, target))
            return 0

        lax.fori_loop(0, 7, send, 0)

        @pl.when(my_chunk != chunk)
        def _():
            send(jnp.int32(7), 0)

        @pl.when(my_chunk == chunk)
        def _():
            field, height, _unused = place(jnp.int32(7))
            each(field, height, stay)

    def ring_wait(step, ring):
        pltpu.make_async_copy(ring, ring, ring_sems.at[step]).wait()

    def sweep(step, ring, swept):
        def one(r, _):
            x = ring[pl.ds(r, n_phi, stride=RADIAL), :]
            offset = offsets[step, r]
            hops = lax.shift_right_logical(offset, 7)
            rest = jnp.bitwise_and(offset, 127)
            x = pltpu.roll(x, hops, 0)
            x = pltpu.roll(x, rest, 1)
            x = jnp.where(lane >= rest, x, pltpu.roll(x, 1, 0))
            before = pltpu.roll(x, 1, 0)
            after = pltpu.roll(x, n_phi - 1, 0)

            def back(k):
                return pltpu.roll(jnp.where(lane < LANES - k, x, before), k, 1)

            def ahead(k):
                return pltpu.roll(jnp.where(lane >= k, x, after), LANES - k, 1)

            m1, m2, m3 = back(1), back(2), back(3)
            p1, p2, p3 = ahead(1), ahead(2), ahead(3)
            c = jnp.full((n_phi, LANES), courants[step, r], jnp.float32)
            size = jnp.abs(c)
            upwind = c >= 0.0
            f_m2 = face_value(m3, m2, m1, x)
            f_m1 = face_value(m2, m1, x, p1)
            f_0 = face_value(m1, x, p1, p2)
            f_p1 = face_value(x, p1, p2, p3)
            inner = 1.0 - size * (2.0 / 3.0)

            def flux(face, low_face, high_face, low, high):
                other = jnp.where(upwind, low_face, high_face)
                base = jnp.where(upwind, low, high)
                bend = 6.0 * base - 3.0 * (other + face)
                return face - 0.5 * size * ((face - other) - inner * bend)

            change = flux(f_0, f_m1, f_p1, x, p1) - flux(f_m1, f_m2, f_0, m1, x)
            swept[pl.ds(r, n_phi, stride=RADIAL), :] = x - c * change
            return 0

        lax.fori_loop(0, RADIAL, one, 0, unroll=2)

    def to_home(step, swept, home):
        landing = home.at[pl.ds(my_slab * SLAB + PAD, RADIAL)]
        arrival = home_sems.at[step * CHUNKS + my_chunk]

        def send(i, _):
            target = far_first(i)
            pltpu.make_async_remote_copy(
                src_ref=swept.at[pl.ds(target * RADIAL, RADIAL)],
                dst_ref=landing,
                send_sem=send_sems.at[2 * step + 1],
                recv_sem=arrival,
                device_id={"phi": target},
                device_id_type=MESH,
            ).start()
            return 0

        lax.fori_loop(1, n_phi, send, 0)
        pltpu.make_async_copy(swept.at[pl.ds(me * RADIAL, RADIAL)], landing, arrival).start()

    def home_wait(step, chunk):
        block = swept_a.at[pl.ds(0, 8 * RADIAL)]
        pltpu.make_async_copy(block, block, home_sems.at[step * CHUNKS + chunk]).wait()

    def rims(step, chunk, home):
        slabs = home.reshape(FIELDS * nz, SLAB, LANES)
        base = 2 * (step * CHUNKS + chunk)

        def copy(src, dst, sem, target):
            return pltpu.make_async_remote_copy(
                src_ref=slabs.at[pl.ds(8 * chunk, 8), pl.ds(src, 3), :],
                dst_ref=slabs.at[pl.ds(8 * chunk, 8), pl.ds(dst, 3), :],
                send_sem=rim_send_sems.at[base + sem],
                recv_sem=rim_sems.at[base + sem],
                device_id={"row": target},
                device_id_type=MESH,
            )

        up = copy(PAD + RADIAL - 3, PAD - 3, 0, tile + 1)
        down = copy(PAD, PAD + RADIAL, 1, tile - 1)
        return up, down

    def rims_start(step, chunk, home):
        up, down = rims(step, chunk, home)

        @pl.when(jnp.logical_not(at_end))
        def _():
            up.start()

        @pl.when(jnp.logical_not(at_start))
        def _():
            down.start()

        def rows(index):
            return pl.ds(8 * chunk * SLAB + index, 8, stride=SLAB)

        @pl.when(at_start)
        def _():
            for j in range(3):
                home[rows(PAD - 3 + j), :] = home[rows(PAD), :]

        @pl.when(at_end)
        def _():
            for j in range(3):
                home[rows(PAD + RADIAL + j), :] = home[rows(PAD + RADIAL - 1), :]

    def rims_wait(step, chunk, home):
        up, down = rims(step, chunk, home)

        @pl.when(jnp.logical_not(at_end))
        def _():
            up.wait_send()
            down.wait_recv()

        @pl.when(jnp.logical_not(at_start))
        def _():
            down.wait_send()
            up.wait_recv()

    def turned(x, by):
        return pltpu.roll(x, by % 8, 0)

    def everywhere(x, field):
        x = turned(x, -field) if field else x
        x = jnp.where(part == 0, x, 0.0)
        x = x + turned(x, 1)
        return x + turned(x, 2)

    def two_sums(first, second):
        pairs = jnp.where(even, first + turned(first, -1), turned(second + turned(second, -1), 1))
        return pairs + turned(pairs, -2)

    def finish(step, chunk, home):
        last = step == STEPS - 1

        def gas_rows(index):
            return home[pl.ds(8 * chunk * SLAB + index, 8, stride=SLAB), :]

        def flux(low, high, low_face, face, high_face, c):
            size = jnp.abs(c)
            upwind = c >= 0.0
            other = jnp.where(upwind, low_face, high_face)
            base = jnp.where(upwind, low, high)
            bend = 6.0 * base - 3.0 * (other + face)
            inner = 1.0 - size * (2.0 / 3.0)
            return c * (face - 0.5 * size * ((face - other) - inner * bend))

        start = [gas_rows(PAD - 3 + j) for j in range(6)]
        face_0 = face_value(*start[0:4])
        face_1 = face_value(*start[1:5])
        face_2 = face_value(*start[2:6])
        speed_0 = radial_rate * everywhere(start[2], 1)
        speed_1 = radial_rate * everywhere(start[3], 1)
        first = flux(start[2], start[3], face_0, face_1, face_2, speed_0 + speed_1)

        def one(r, carry):
            low_flux, face_low, face, cell, next1, next2, speed = carry
            next3 = gas_rows(r + (PAD + 3))
            speed_high = radial_rate * everywhere(next1, 1)
            face_high = face_value(cell, next1, next2, next3)
            high_flux = flux(cell, next1, face_low, face, face_high, speed + speed_high)
            gas = cell - (high_flux - low_flux)
            floored = jnp.maximum(everywhere(gas, 0), density_floor)
            u_r = everywhere(gas, 1)
            u_p = everywhere(gas, 2)
            here = pl.ds(pl.multiple_of(r * FIELDS * nz + 8 * chunk, 8), 8)
            weight = live_mass[here, :]
            v_r = slot_radial[here, :]
            v_p = slot_azimuth[here, :]
            drag = floored * slot_stop[here, :]
            drag = drag / (1.0 + drag)
            d_r = drag * (u_r - v_r)
            d_p = drag * (u_p - v_p)
            kicks = turned(two_sums(weight * d_r, weight * d_p), 1) / floored
            gas = gas - jnp.where(jnp.logical_or(part == 1, part == 2), kicks, 0.0)
            v_r = v_r + d_r
            v_p = v_p + d_p
            spread = pl.ds(8 * chunk * RADIAL + r, 8, stride=RADIAL)
            if last:
                stays = stay_mass[here, :]
                goes = weight - stays
                kept = two_sums(stays * v_r, stays * v_p)
                gone = turned(two_sums(goes * v_r, goes * v_p), 2)
                push[spread, :] = jnp.where(part < 2, kept, gone)
                final[spread, :] = gas
            else:
                slot_radial[here, :] = v_r
                slot_azimuth[here, :] = v_p
                leave[spread, :] = gas
            return (high_flux, face, face_high, next1, next2, next3, speed_high)

        lax.fori_loop(
            0,
            RADIAL,
            one,
            (first, face_1, face_2, start[3], start[4], start[5], speed_1),
            unroll=2,
        )

    def blocks(value):
        return value.reshape(slab_rows // 8, 8, LANES)

    def plan():
        def one(r, _):
            rows = pl.ds(r, nz, stride=RADIAL)
            live_count = occ[rows, :]
            stay_count = live_count - move[rows, :]
            kept_mass = jnp.zeros((nz, LANES), jnp.float32)
            moved_mass = jnp.zeros((nz, LANES), jnp.float32)
            for k in range(K):
                source = pl.ds(k * slab_rows + r, nz, stride=RADIAL)
                target = pl.ds(r * nz * K + k, nz, stride=K)
                weight = mass[source, :]
                live = jnp.where(k < live_count, weight, 0.0)
                stays = jnp.where(k < stay_count, weight, 0.0)
                kept_mass = kept_mass + stays
                moved_mass = moved_mass + jnp.where(k < stay_count, 0.0, live)
                live_mass[target, :] = live
                stay_mass[target, :] = stays
                slot_stop[target, :] = stop[source, :]
                slot_radial[target, :] = dust[source, :]
                slot_azimuth[target, :] = dust[
                    pl.ds((K + k) * slab_rows + r, nz, stride=RADIAL), :
                ]
            grid[0, rows, :] = kept_mass
            leaving_mass[rows, :] = moved_mass
            return 0

        lax.fori_loop(0, RADIAL, one, 0)
        has = blocks(move[...]) > 0
        starts, ends = move_plan(has)
        picks[...] = ends.reshape(slab_rows, LANES)
        marks = jnp.where(has, 1 << HAS_BIT, 0) + blocks(dest[...]) * (1 << DEST_BIT)
        route[...] = jnp.bitwise_or(starts, marks).reshape(slab_rows, LANES)
        (listed,) = compact([blocks(leaving_mass[...])], ends)
        mass_list[...] = listed.reshape(LIST, LANES)

    def to_tiles(pairs):
        def send(i, _):
            target = lax.rem(tile + i, n_row)
            for number, source, landing in pairs:
                count = source.shape[0]
                pltpu.make_async_remote_copy(
                    src_ref=source,
                    dst_ref=landing.at[pl.ds(tile * count, count)],
                    send_sem=list_send_sems.at[number],
                    recv_sem=list_sems.at[number],
                    device_id={"row": target},
                    device_id_type=MESH,
                ).start()
            return 0

        lax.fori_loop(1, n_row, send, 0)

    def tiles_wait(pairs, sems):
        for number, source, landing in pairs:
            piece = landing.at[pl.ds(0, (n_row - 1) * source.shape[0])]
            pltpu.make_async_copy(piece, piece, sems.at[number]).wait()

    def gather(number, landing, count):
        def one(i, _):
            source = lax.rem(tile + i, n_row)
            code = blocks(routes[pl.ds(source * slab_rows, slab_rows), :])
            lists = [
                landing[pl.ds((source * count + j) * LIST, LIST), :].reshape(LIST // 8, 8, LANES)
                for j in range(count)
            ]
            spread = expand(lists, code, slab_rows // 8)
            wanted = lax.shift_right_logical(code, DEST_BIT) == tile + (1 << (HAS_BIT - DEST_BIT))
            for j in range(count):
                added = jnp.where(wanted, spread[j], 0.0).reshape(slab_rows, LANES)
                grid[number + j] = grid[number + j] + added
            return 0

        lax.fori_loop(1, n_row, one, 0)

    early = ((0, route, routes), (1, mass_list, mass_lists))
    late = ((2, push_list, push_lists),)

    for chunk in range(CHUNKS):
        to_ring(0, chunk, ring_a)
    for load in loads:
        load.wait()
    plan()
    to_tiles(early)
    for step, ring, swept, home in ((0, ring_a, swept_a, home_a), (1, ring_b, swept_b, home_b)):
        ring_wait(step, ring)
        sweep(step, ring, swept)
        to_home(step, swept, home)
        for chunk in range(CHUNKS):
            home_wait(step, chunk)
            rims_start(step, chunk, home)
        for chunk in range(CHUNKS):
            rims_wait(step, chunk, home)
            finish(step, chunk, home)
            if step + 1 < STEPS:
                to_ring(step + 1, chunk, ring_b)
        if step == 0:
            tiles_wait(early, list_sems)
            gather(0, mass_lists, 1)
    parted = push.reshape(nz, FIELDS, RADIAL, LANES)
    pushes = compact([blocks(parted[:, 2]), blocks(parted[:, 3])], blocks(picks[...]))
    push_list[pl.ds(0, LIST), :] = pushes[0].reshape(LIST, LANES)
    push_list[pl.ds(LIST, LIST), :] = pushes[1].reshape(LIST, LANES)
    to_tiles(late)
    store = pltpu.make_async_copy(final, gas_out, store_sems.at[0])
    store.start()
    grid[1] = parted[:, 0].reshape(slab_rows, LANES)
    grid[2] = parted[:, 1].reshape(slab_rows, LANES)
    tiles_wait(late, list_sems)
    gather(1, push_lists, 2)
    result = pltpu.make_async_copy(grid, dust_out, store_sems.at[1])
    result.start()
    tiles_wait(early, list_send_sems)
    tiles_wait(late, list_send_sems)
    partners = (n_phi - 1) * RADIAL
    for i in range(2 * STEPS):
        pltpu.make_async_copy(
            swept_a.at[pl.ds(0, partners)], swept_a.at[pl.ds(0, partners)], send_sems.at[i]
        ).wait()
    store.wait()
    result.wait()


def copy_kernel(gas, dust, density_out, velocity_out, dust_out, sems):
    copies = [
        pltpu.make_async_copy(gas.at[:, 0], density_out, sems.at[0]),
        pltpu.make_async_copy(dust, dust_out, sems.at[1]),
    ] + [pltpu.make_async_copy(gas.at[:, 1 + i], velocity_out.at[i], sems.at[2 + i]) for i in range(3)]
    for copy in copies:
        copy.start()
    for copy in copies:
        copy.wait()


def gas_and_dust(density, velocity, offsets, courants, mass, stop, dust_velocity, occ, move, dest):
    n_phi = lax.axis_size("phi")
    n_row = lax.axis_size("row")
    nz, radial, lanes = density.shape
    cells = nz * radial

    def flat(array):
        return array.reshape(-1, lanes)

    def rows(count, dtype=jnp.float32):
        return pltpu.VMEM((count, lanes), dtype)

    hbm = pl.BlockSpec(memory_space=pltpu.HBM)
    smem = pl.BlockSpec(memory_space=pltpu.SMEM)
    dma = pltpu.SemaphoreType.DMA
    ring = n_phi * radial
    gas, dust = pl.pallas_call(
        functools.partial(gas_kernel, n_phi, n_row, nz),
        out_shape=(
            jax.ShapeDtypeStruct((FIELDS * cells, lanes), jnp.float32),
            jax.ShapeDtypeStruct((3, cells, lanes), jnp.float32),
        ),
        in_specs=[hbm, hbm, smem, smem] + [hbm] * 6,
        out_specs=[hbm] * 2,
        scratch_shapes=[
            rows(ring),
            rows(ring),
            rows(ring),
            rows(ring),
            rows(FIELDS * nz * SLAB),
            rows(FIELDS * nz * SLAB),
            rows(FIELDS * cells),
            rows(FIELDS * cells),
            rows(K * cells),
            rows(K * cells),
            rows(2 * K * cells),
            rows(cells, jnp.int32),
            rows(cells, jnp.int32),
            rows(cells, jnp.int32),
            rows(K * cells),
            rows(K * cells),
            rows(K * cells),
            rows(K * cells),
            rows(K * cells),
            rows(cells, jnp.int32),
            rows(cells, jnp.int32),
            rows(n_row * cells, jnp.int32),
            rows(LIST),
            rows(n_row * LIST),
            rows(2 * LIST),
            rows(2 * n_row * LIST),
            rows(cells),
            rows(FIELDS * cells),
            pltpu.VMEM((3, cells, lanes), jnp.float32),
            dma((2 * STEPS,)),
            dma((STEPS,)),
            dma((STEPS * CHUNKS,)),
            dma((2 * STEPS * CHUNKS,)),
            dma((2 * STEPS * CHUNKS,)),
            dma((3,)),
            dma((3,)),
            dma((6,)),
            dma((2,)),
        ],
        compiler_params=pltpu.CompilerParams(
            collective_id=0, has_side_effects=True, vmem_limit_bytes=56 * 1024 * 1024
        ),
    )(
        flat(density),
        flat(velocity),
        offsets,
        courants,
        flat(mass),
        flat(stop),
        flat(dust_velocity),
        flat(occ),
        flat(move),
        flat(dest),
    )
    return pl.pallas_call(
        copy_kernel,
        out_shape=(
            jax.ShapeDtypeStruct((nz, radial, lanes), jnp.float32),
            jax.ShapeDtypeStruct((3, nz, radial, lanes), jnp.float32),
            jax.ShapeDtypeStruct((3, nz, radial, lanes), jnp.float32),
        ),
        in_specs=[hbm] * 2,
        out_specs=[hbm] * 3,
        scratch_shapes=[dma((5,))],
        compiler_params=pltpu.CompilerParams(vmem_limit_bytes=56 * 1024 * 1024),
    )(gas.reshape(nz, FIELDS, radial, lanes), dust.reshape(3, nz, radial, lanes))


def body(
    gas_density,
    gas_velocity,
    orbital_offsets,
    residual_courant,
    dust_mass,
    dust_stop,
    dust_velocity,
    occupancy,
    move_count,
    dest_tile,
):
    return gas_and_dust(
        gas_density,
        gas_velocity,
        orbital_offsets,
        residual_courant,
        dust_mass,
        dust_stop,
        dust_velocity,
        occupancy,
        move_count,
        dest_tile,
    )


def solution(mesh):
    return jax.shard_map(
        body,
        mesh=mesh,
        in_specs=(
            P(None, "row", "phi"),
            P(None, None, "row", "phi"),
            P(None, "row"),
            P(None, "row"),
            P(None, None, "row", "phi"),
            P(None, None, "row", "phi"),
            P(None, None, None, "row", "phi"),
            P(None, "row", "phi"),
            P(None, "row", "phi"),
            P(None, "row", "phi"),
        ),
        out_specs=(P(None, "row", "phi"), P(None, None, "row", "phi"), P(None, None, "row", "phi")),
        check_vma=False,
    )
```

time: 82.3 us -> 85.9 us (1.044)
  Pallas kernels: 77.7 us -> 85.1 us
  local copies, waits for them, and re-layouts: 3.81 us -> 0 us
    pallas_call x0 -> x1, Pallas kernels: none -> 15 us  [gas_and_dust(): pl.pallas_call(copy_kernel, out_shape=(jax.ShapeDtypeStruct((nz, radial,...]
    pallas_call x1, Pallas kernels: 77.7 us -> 70.1 us  [gas_and_dust(): pl.pallas_call(functools.partial(gas_kernel, n_phi, n_row, nz), out_shape...]
    unnamed x5 -> x0, local copies, waits for them, and re-layouts: 3.81 us -> none
where the time goes in v3:
time: 85.9 us; the launch traced here: 85.8 us
  Pallas kernels  85.1 us (99%)
    pallas_call x1, Pallas kernels, gas_and_dust(): pl.pallas_call(functools.partial(gas_kernel, n_phi, n_row, nz), out_shape...  70.1 us
    pallas_call x1, Pallas kernels, gas_and_dust(): pl.pallas_call(copy_kernel, out_shape=(jax.ShapeDtypeStruct((nz, radial,...  15 us

profile of v3, /device:TPU:8, one launch (start us, length us, event | category | flops | bytes accessed | tf_op | source)
XLA Modules:
  0.0 85.8 jit_solution(1689791969262508014)
XLA Ops:
  0.6 70.1 %shard_map.121 = (f32[512,128]{1,0:T(8,128)}, f32[3,128,128]{2,1,0:T(8,128)}) custom-call(f32[128,128]{1,0:T(8,128)} %bitcast.16, f32[384,128]{1,0:T(8,128)} %bitcast.15, s32[2,16]{1,0:T(2,128)} %offsets.1, f32[2,16]{1,0:T(2,128)} %courants.1, f32[512,128]{1,0:T(8,128)} %bitcast.12, f32[512,128]{1,0:T(8,128)} %bitcast.13, f32[1024,128]{1,0:T(8,128)} %bitcast.10, ...), custom_call_target="tpu_custom_call" | custom-call | tf_op jit(solution)/shard_map/pallas_call | solution.py:645
  70.7 15.0 %shard_map.122 = (f32[8,16,128]{2,1,0:T(8,128)}, f32[3,8,16,128]{3,2,1,0:T(8,128)}, f32[3,8,16,128]{3,2,1,0:T(8,128)}) custom-call(f32[8,4,16,128]{3,2,1,0:T(8,128)} %bitcast.11, f32[3,8,16,128]{3,2,1,0:T(8,128)} %bitcast.14), custom_call_target="tpu_custom_call" | custom-call | tf_op jit(solution)/shard_map/pallas_call | solution.py:708

commit v4 on v3

--- a/solution.py
+++ b/solution.py
@@ -23,6 +23,7 @@
 HAS_BIT = 17
 BITS = 14
 CHUNKS = 4
+VMEM_BYTES = 56 * 1024 * 1024
 MESH = pl.DeviceIdType.MESH
 
 
@@ -135,8 +136,8 @@
     occ_in,
     move_in,
     dest_in,
-    gas_out,
-    dust_out,
+    final,
+    grid,
     ring_a,
     ring_b,
     swept_a,
@@ -144,7 +145,6 @@
     home_a,
     home_b,
     leave,
-    final,
     mass,
     stop,
     dust,
@@ -165,7 +165,6 @@
     push_lists,
     leaving_mass,
     push,
-    grid,
     send_sems,
     ring_sems,
     home_sems,
@@ -174,7 +173,6 @@
     list_send_sems,
     list_sems,
     load_sems,
-    store_sems,
 ):
     me = lax.axis_index("phi")
     tile = lax.axis_index("row")
@@ -596,14 +594,10 @@
     push_list[pl.ds(0, LIST), :] = pushes[0].reshape(LIST, LANES)
     push_list[pl.ds(LIST, LIST), :] = pushes[1].reshape(LIST, LANES)
     to_tiles(late)
-    store = pltpu.make_async_copy(final, gas_out, store_sems.at[0])
-    store.start()
     grid[1] = parted[:, 0].reshape(slab_rows, LANES)
     grid[2] = parted[:, 1].reshape(slab_rows, LANES)
     tiles_wait(late, list_sems)
     gather(1, push_lists, 2)
-    result = pltpu.make_async_copy(grid, dust_out, store_sems.at[1])
-    result.start()
     tiles_wait(early, list_send_sems)
     tiles_wait(late, list_send_sems)
     partners = (n_phi - 1) * RADIAL
@@ -611,15 +605,16 @@
         pltpu.make_async_copy(
             swept_a.at[pl.ds(0, partners)], swept_a.at[pl.ds(0, partners)], send_sems.at[i]
         ).wait()
-    store.wait()
-    result.wait()
 
 
 def copy_kernel(gas, dust, density_out, velocity_out, dust_out, sems):
     copies = [
         pltpu.make_async_copy(gas.at[:, 0], density_out, sems.at[0]),
         pltpu.make_async_copy(dust, dust_out, sems.at[1]),
-    ] + [pltpu.make_async_copy(gas.at[:, 1 + i], velocity_out.at[i], sems.at[2 + i]) for i in range(3)]
+    ] + [
+        pltpu.make_async_copy(gas.at[:, 1 + i], velocity_out.at[i], sems.at[2 + i])
+        for i in range(3)
+    ]
     for copy in copies:
         copy.start()
     for copy in copies:
@@ -639,17 +634,18 @@
         return pltpu.VMEM((count, lanes), dtype)
 
     hbm = pl.BlockSpec(memory_space=pltpu.HBM)
+    vmem = pl.BlockSpec(memory_space=pltpu.VMEM)
     smem = pl.BlockSpec(memory_space=pltpu.SMEM)
     dma = pltpu.SemaphoreType.DMA
     ring = n_phi * radial
     gas, dust = pl.pallas_call(
         functools.partial(gas_kernel, n_phi, n_row, nz),
         out_shape=(
-            jax.ShapeDtypeStruct((FIELDS * cells, lanes), jnp.float32),
-            jax.ShapeDtypeStruct((3, cells, lanes), jnp.float32),
+            pltpu.VMEM((FIELDS * cells, lanes), jnp.float32),
+            pltpu.VMEM((3, cells, lanes), jnp.float32),
         ),
         in_specs=[hbm, hbm, smem, smem] + [hbm] * 6,
-        out_specs=[hbm] * 2,
+        out_specs=[vmem] * 2,
         scratch_shapes=[
             rows(ring),
             rows(ring),
@@ -657,7 +653,6 @@
             rows(ring),
             rows(FIELDS * nz * SLAB),
             rows(FIELDS * nz * SLAB),
-            rows(FIELDS * cells),
             rows(FIELDS * cells),
             rows(K * cells),
             rows(K * cells),
@@ -679,7 +674,6 @@
             rows(2 * n_row * LIST),
             rows(cells),
             rows(FIELDS * cells),
-            pltpu.VMEM((3, cells, lanes), jnp.float32),
             dma((2 * STEPS,)),
             dma((STEPS,)),
             dma((STEPS * CHUNKS,)),
@@ -688,10 +682,9 @@
             dma((3,)),
             dma((3,)),
             dma((6,)),
-            dma((2,)),
         ],
         compiler_params=pltpu.CompilerParams(
-            collective_id=0, has_side_effects=True, vmem_limit_bytes=56 * 1024 * 1024
+            collective_id=0, has_side_effects=True, vmem_limit_bytes=VMEM_BYTES
         ),
     )(
         flat(density),
@@ -712,10 +705,9 @@
             jax.ShapeDtypeStruct((3, nz, radial, lanes), jnp.float32),
             jax.ShapeDtypeStruct((3, nz, radial, lanes), jnp.float32),
         ),
-        in_specs=[hbm] * 2,
+        in_specs=[vmem] * 2,
         out_specs=[hbm] * 3,
         scratch_shapes=[dma((5,))],
-        compiler_params=pltpu.CompilerParams(vmem_limit_bytes=56 * 1024 * 1024),
     )(gas.reshape(nz, FIELDS, radial, lanes), dust.reshape(3, nz, radial, lanes))
 
 

time: 85.9 us -> 73.3 us (0.85)
  Pallas kernels: 85.1 us -> 71.2 us
  local copies, waits for them, and re-layouts: 0 us -> 1.37 us
    pallas_call x1, Pallas kernels: 15 us -> 1.81 us  [gas_and_dust(): pl.pallas_call(copy_kernel, out_shape=(jax.ShapeDtypeStruct((nz, radial,...]
    unnamed x0 -> x4, local copies, waits for them, and re-layouts: none -> 1.37 us
where the time goes in v4:
time: 73.3 us; the launch traced here: 73.2 us
  Pallas kernels  71.2 us (97%)
  local copies, waits for them, and re-layouts  1.37 us (2%)
    pallas_call x1, Pallas kernels, gas_and_dust(): pl.pallas_call(functools.partial(gas_kernel, n_phi, n_row, nz), out_shape...  69.4 us
    pallas_call x1, Pallas kernels, gas_and_dust(): pl.pallas_call(copy_kernel, out_shape=(jax.ShapeDtypeStruct((nz, radial,...  1.81 us

profile of v4, /device:TPU:8, one launch (start us, length us, event | category | flops | bytes accessed | tf_op | source)
XLA Modules:
  0.0 73.2 jit_solution(10252162234613378704)
XLA Ops:
  0.6 69.4 %shard_map.121 = (f32[512,128]{1,0:T(8,128)S(1)}, f32[3,128,128]{2,1,0:T(8,128)S(1)}) custom-call(f32[128,128]{1,0:T(8,128)} %bitcast.16, f32[384,128]{1,0:T(8,128)} %bitcast.15, s32[2,16]{1,0:T(2,128)} %offsets.1, f32[2,16]{1,0:T(2,128)} %courants.1, f32[512,128]{1,0:T(8,128)} %bitcast.13, f32[512,128]{1,0:T(8,128)} %bitcast.14, f32[1024,128]{1,0:T(8,128)} %bitcast.12, ...), custom_call_target="tpu_custom_call" | custom-call | tf_op jit(solution)/shard_map/pallas_call | solution.py:641
  70.0 0.0 copy-start
  70.1 0.7 copy-done
  70.7 0.0 copy-start.1
  70.7 0.7 copy-done.1
  71.4 1.8 %shard_map.122 = (f32[8,16,128]{2,1,0:T(8,128)}, f32[3,8,16,128]{3,2,1,0:T(8,128)}, f32[3,8,16,128]{3,2,1,0:T(8,128)}) custom-call(f32[8,4,16,128]{3,2,1,0:T(8,128)} %bitcast.10, f32[3,8,16,128]{3,2,1,0:T(8,128)} %bitcast.11), custom_call_target="tpu_custom_call" | custom-call | tf_op jit(solution)/shard_map/pallas_call | solution.py:701
Async XLA Ops:
  70.0 0.7 copy-start
  70.7 0.7 copy-start.1

commit v5 on v4

--- a/solution.py
+++ b/solution.py
@@ -24,6 +24,7 @@
 BITS = 14
 CHUNKS = 4
 VMEM_BYTES = 56 * 1024 * 1024
+COPY_VMEM_BYTES = 2 * 1024 * 1024
 MESH = pl.DeviceIdType.MESH
 
 
@@ -172,6 +173,8 @@
     rim_send_sems,
     list_send_sems,
     list_sems,
+    push_send_sem,
+    push_sems,
     load_sems,
 ):
     me = lax.axis_index("phi")
@@ -182,7 +185,7 @@
     my_chip = lax.shift_right_logical(me, 2)
     my_side = jnp.bitwise_and(lax.shift_right_logical(me, 1), 1)
     my_core = jnp.bitwise_and(me, 1)
-    my_chunk = 2 * jnp.bitwise_and(my_chip, 1) + my_core
+    my_chunk = 2 * my_core + jnp.bitwise_and(my_chip, 1)
     my_field = lax.shift_right_logical(my_chip, 1)
     my_slab = 8 * my_chunk + 4 * my_side + my_field
 
@@ -251,7 +254,7 @@
             turn = jnp.bitwise_xor(2, jnp.bitwise_xor(pair, lax.shift_right_logical(pair, 1)))
             field = jnp.bitwise_xor(my_field, turn)
             side = jnp.bitwise_xor(my_side, jnp.bitwise_xor(jnp.bitwise_and(j, 1), 1))
-            target = (2 * field + chunk // 2) * 4 + 2 * side + chunk % 2
+            target = (2 * field + chunk % 2) * 4 + 2 * side + chunk // 2
             return field, 2 * chunk + side, target
 
         def rows(ref, index):
@@ -526,6 +529,35 @@
         (listed,) = compact([blocks(leaving_mass[...])], ends)
         mass_list[...] = listed.reshape(LIST, LANES)
 
+    def table(j, values):
+        value = jnp.int32(values[0])
+        for index in range(1, len(values)):
+            value = jnp.where(j == index, values[index], value)
+        return value
+
+    def neighbour(j, sign):
+        column = lax.shift_right_logical(tile, 1) + 4 + sign * table(j, (0, 1, -1, 1, -1, 2, 2))
+        side = jnp.bitwise_xor(jnp.bitwise_and(tile, 1), table(j, (1, 0, 0, 1, 1, 0, 1)))
+        return 2 * jnp.bitwise_and(column, 3) + side
+
+    def push_copy(j, target):
+        return pltpu.make_async_remote_copy(
+            src_ref=push_list,
+            dst_ref=push_lists.at[pl.ds(tile * 2 * LIST, 2 * LIST)],
+            send_sem=push_send_sem.at[0],
+            recv_sem=push_sems.at[j],
+            device_id={"row": target},
+            device_id_type=MESH,
+        )
+
+    def push_start():
+        def send(i, _):
+            j = n_row - 2 - i
+            push_copy(j, neighbour(j, 1)).start()
+            return 0
+
+        lax.fori_loop(0, n_row - 1, send, 0)
+
     def to_tiles(pairs):
         def send(i, _):
             target = lax.rem(tile + i, n_row)
@@ -548,25 +580,35 @@
             piece = landing.at[pl.ds(0, (n_row - 1) * source.shape[0])]
             pltpu.make_async_copy(piece, piece, sems.at[number]).wait()
 
-    def gather(number, landing, count):
+    def add(number, landing, count, source):
+        code = blocks(routes[pl.ds(source * slab_rows, slab_rows), :])
+        lists = [
+            landing[pl.ds((source * count + j) * LIST, LIST), :].reshape(LIST // 8, 8, LANES)
+            for j in range(count)
+        ]
+        spread = expand(lists, code, slab_rows // 8)
+        wanted = lax.shift_right_logical(code, DEST_BIT) == tile + (1 << (HAS_BIT - DEST_BIT))
+        for j in range(count):
+            added = jnp.where(wanted, spread[j], 0.0).reshape(slab_rows, LANES)
+            grid[number + j] = grid[number + j] + added
+
+    def gather_mass():
         def one(i, _):
-            source = lax.rem(tile + i, n_row)
-            code = blocks(routes[pl.ds(source * slab_rows, slab_rows), :])
-            lists = [
-                landing[pl.ds((source * count + j) * LIST, LIST), :].reshape(LIST // 8, 8, LANES)
-                for j in range(count)
-            ]
-            spread = expand(lists, code, slab_rows // 8)
-            wanted = lax.shift_right_logical(code, DEST_BIT) == tile + (1 << (HAS_BIT - DEST_BIT))
-            for j in range(count):
-                added = jnp.where(wanted, spread[j], 0.0).reshape(slab_rows, LANES)
-                grid[number + j] = grid[number + j] + added
+            add(0, mass_lists, 1, lax.rem(tile + i, n_row))
             return 0
 
         lax.fori_loop(1, n_row, one, 0)
 
+    def gather_push():
+        def one(j, _):
+            source = neighbour(j, -1)
+            push_copy(j, source).wait_recv()
+            add(1, push_lists, 2, source)
+            return 0
+
+        lax.fori_loop(0, n_row - 1, one, 0)
+
     early = ((0, route, routes), (1, mass_list, mass_lists))
-    late = ((2, push_list, push_lists),)
 
     for chunk in range(CHUNKS):
         to_ring(0, chunk, ring_a)
@@ -578,6 +620,9 @@
         ring_wait(step, ring)
         sweep(step, ring, swept)
         to_home(step, swept, home)
+        if step == 1:
+            tiles_wait(early, list_sems)
+            gather_mass()
         for chunk in range(CHUNKS):
             home_wait(step, chunk)
             rims_start(step, chunk, home)
@@ -586,20 +631,17 @@
             finish(step, chunk, home)
             if step + 1 < STEPS:
                 to_ring(step + 1, chunk, ring_b)
-        if step == 0:
-            tiles_wait(early, list_sems)
-            gather(0, mass_lists, 1)
     parted = push.reshape(nz, FIELDS, RADIAL, LANES)
     pushes = compact([blocks(parted[:, 2]), blocks(parted[:, 3])], blocks(picks[...]))
     push_list[pl.ds(0, LIST), :] = pushes[0].reshape(LIST, LANES)
     push_list[pl.ds(LIST, LIST), :] = pushes[1].reshape(LIST, LANES)
-    to_tiles(late)
+    push_start()
     grid[1] = parted[:, 0].reshape(slab_rows, LANES)
     grid[2] = parted[:, 1].reshape(slab_rows, LANES)
-    tiles_wait(late, list_sems)
-    gather(1, push_lists, 2)
+    gather_push()
     tiles_wait(early, list_send_sems)
-    tiles_wait(late, list_send_sems)
+    sent = push_lists.at[pl.ds(0, (n_row - 1) * 2 * LIST)]
+    pltpu.make_async_copy(sent, sent, push_send_sem.at[0]).wait()
     partners = (n_phi - 1) * RADIAL
     for i in range(2 * STEPS):
         pltpu.make_async_copy(
@@ -679,8 +721,10 @@
             dma((STEPS * CHUNKS,)),
             dma((2 * STEPS * CHUNKS,)),
             dma((2 * STEPS * CHUNKS,)),
-            dma((3,)),
-            dma((3,)),
+            dma((2,)),
+            dma((2,)),
+            dma((1,)),
+            dma((n_row - 1,)),
             dma((6,)),
         ],
         compiler_params=pltpu.CompilerParams(
@@ -708,6 +752,7 @@
         in_specs=[vmem] * 2,
         out_specs=[hbm] * 3,
         scratch_shapes=[dma((5,))],
+        compiler_params=pltpu.CompilerParams(vmem_limit_bytes=COPY_VMEM_BYTES),
     )(gas.reshape(nz, FIELDS, radial, lanes), dust.reshape(3, nz, radial, lanes))
 
 

time: 73.3 us -> 67.4 us (0.920)
  Pallas kernels: 71.2 us -> 66.5 us
  local copies, waits for them, and re-layouts: 1.37 us -> 0 us
    pallas_call x1, Pallas kernels: 69.4 us -> 65.7 us  [gas_and_dust(): pl.pallas_call(functools.partial(gas_kernel, n_phi, n_row, nz), out_shape...]
    unnamed x4 -> x0, local copies, waits for them, and re-layouts: 1.37 us -> none
    pallas_call x1, Pallas kernels: 1.81 us -> 0.8 us  [gas_and_dust(): pl.pallas_call(copy_kernel, out_shape=(jax.ShapeDtypeStruct((nz, radial,...]
where the time goes in v5:
time: 67.4 us; the launch traced here: 67.2 us
  Pallas kernels  66.5 us (99%)
    pallas_call x1, Pallas kernels, gas_and_dust(): pl.pallas_call(functools.partial(gas_kernel, n_phi, n_row, nz), out_shape...  65.7 us

profile of v5, /device:TPU:8, one launch (start us, length us, event | category | flops | bytes accessed | tf_op | source)
XLA Modules:
  0.0 67.2 jit_solution(7925705599778916442)
XLA Ops:
  0.6 65.7 %shard_map.121 = (f32[512,128]{1,0:T(8,128)S(1)}, f32[3,128,128]{2,1,0:T(8,128)S(1)}) custom-call(f32[128,128]{1,0:T(8,128)} %bitcast.16, f32[384,128]{1,0:T(8,128)} %bitcast.15, s32[2,16]{1,0:T(2,128)} %offsets.1, f32[2,16]{1,0:T(2,128)} %courants.1, f32[512,128]{1,0:T(8,128)} %bitcast.13, f32[512,128]{1,0:T(8,128)} %bitcast.14, f32[1024,128]{1,0:T(8,128)} %bitcast.12, ...), custom_call_target="tpu_custom_call" | custom-call | tf_op jit(solution)/shard_map/pallas_call | solution.py:683
  66.4 0.8 %shard_map.122 = (f32[8,16,128]{2,1,0:T(8,128)}, f32[3,8,16,128]{3,2,1,0:T(8,128)}, f32[3,8,16,128]{3,2,1,0:T(8,128)}) custom-call(f32[8,4,16,128]{3,2,1,0:T(8,128)S(1)} %bitcast.10, f32[3,8,16,128]{3,2,1,0:T(8,128)S(1)} %bitcast.11), custom_call_target="tpu_custom_call" | custom-call | tf_op jit(solution)/shard_map/pallas_call | solution.py:745

commit v6 on v5

--- a/solution.py
+++ b/solution.py
@@ -18,7 +18,9 @@
 twelfth = 1.0 / 12.0
 radial_rate = 0.15
 density_floor = 0.5
-LIST = 24
+LIST = 20
+MASS_ROWS = 24
+TAPS = 7
 DEST_BIT = 14
 HAS_BIT = 17
 BITS = 14
@@ -32,94 +34,83 @@
     return (7.0 * (low1 + high1) - (low2 + high2)) * twelfth
 
 
-def indices(shape):
-    return (
-        lax.broadcasted_iota(jnp.int32, shape, 1),
-        lax.broadcasted_iota(jnp.int32, shape, 2),
-    )
-
-
-def later(x, count):
-    return jnp.concatenate([x[count:], jnp.zeros_like(x[:count])], axis=0)
-
-
-def earlier(x, count):
-    return jnp.concatenate([jnp.zeros_like(x[:count]), x[:-count]], axis=0)
-
-
-def moved_down(x, bit):
-    sub, lane = indices(x.shape)
-    if bit >= 10:
-        return later(x, 1 << (bit - 10))
-    if bit >= 3:
-        step = 1 << (bit - 3)
-        return pltpu.roll(jnp.where(lane < step, later(x, 1), x), LANES - step, 2)
+def lanes_of(x):
+    return lax.broadcasted_iota(jnp.int32, x.shape, 1)
+
+
+def moved_down(xs, bit):
+    count = len(xs)
+    if bit >= 11:
+        return [pltpu.roll(x, 8 - (1 << (bit - 11)), 0) for x in xs]
+    if bit >= 7:
+        step = 1 << (bit - 7)
+        return xs[step:] + [pltpu.roll(x, 7, 0) for x in xs[:step]]
     step = 1 << bit
-    turned = pltpu.roll(x, 8 - step, 1)
-    carried = pltpu.roll(jnp.where(lane == 0, later(turned, 1), turned), LANES - 1, 2)
-    return jnp.where(sub < 8 - step, turned, carried)
-
-
-def moved_up(x, bit):
-    sub, lane = indices(x.shape)
-    if bit >= 10:
-        return earlier(x, 1 << (bit - 10))
-    if bit >= 3:
-        step = 1 << (bit - 3)
-        return pltpu.roll(jnp.where(lane >= LANES - step, earlier(x, 1), x), step, 2)
+    lane = lanes_of(xs[0])
+    after = xs[1:] + [pltpu.roll(xs[0], 7, 0)]
+    return [
+        pltpu.roll(jnp.where(lane < step, after[v], xs[v]), LANES - step, 1) for v in range(count)
+    ]
+
+
+def moved_up(xs, bit):
+    count = len(xs)
+    if bit >= 11:
+        return [pltpu.roll(x, 1 << (bit - 11), 0) for x in xs]
+    if bit >= 7:
+        step = 1 << (bit - 7)
+        return [pltpu.roll(x, 1, 0) for x in xs[count - step :]] + xs[: count - step]
     step = 1 << bit
-    turned = pltpu.roll(x, step, 1)
-    carried = pltpu.roll(jnp.where(lane == LANES - 1, earlier(turned, 1), turned), 1, 2)
-    return jnp.where(sub >= step, turned, carried)
+    lane = lanes_of(xs[0])
+    before = [pltpu.roll(xs[-1], 1, 0)] + xs[:-1]
+    return [
+        pltpu.roll(jnp.where(lane >= LANES - step, before[v], xs[v]), step, 1)
+        for v in range(count)
+    ]
 
 
 def has_bit(word, bit):
     return jnp.bitwise_and(word, 1 << bit) != 0
 
 
-def compact(values, picks):
+def chosen_moves(values, words, bits, move):
+    for bit in bits:
+        chosen = [has_bit(word, bit) for word in words]
+        values = [
+            [jnp.where(c, y, x) for c, y, x in zip(chosen, move(xs, bit), xs)] for xs in values
+        ]
+    return values
+
+
+def move_plan(has):
+    lane = lanes_of(has[0])
+    sub = lax.broadcasted_iota(jnp.int32, has[0].shape, 0)
+    empty = [jnp.where(h, 0, 1) for h in has]
+    ahead = empty
+    for step in (1, 2, 4, 8, 16, 32, 64):
+        ahead = [x + jnp.where(lane >= step, pltpu.roll(x, step, 1), 0) for x in ahead]
+    sums = [jnp.zeros_like(empty[0])]
+    for x in ahead:
+        sums.append(sums[-1] + jnp.broadcast_to(x[:, LANES - 1 :], x.shape))
+    whole = sums[-1]
+    for step in (1, 2, 4):
+        whole = whole + jnp.where(sub >= step, pltpu.roll(whole, step, 0), 0)
+    whole = whole - sums[-1]
+    way = [
+        jnp.where(h, x - e + total + whole, 0) for h, x, e, total in zip(has, ahead, empty, sums)
+    ]
+    starts = [jnp.zeros_like(x) for x in way]
+    ends = starts
     for bit in range(BITS):
-        chosen = has_bit(picks, bit)
-        values = [jnp.where(chosen, moved_down(x, bit), x) for x in values]
-    return [x[: LIST // 8] for x in values]
-
-
-def expand(lists, route, blocks):
-    values = [
-        jnp.concatenate([x, jnp.zeros((blocks - LIST // 8, 8, LANES), x.dtype)], axis=0)
-        for x in lists
-    ]
-    for bit in reversed(range(BITS)):
-        chosen = has_bit(route, bit)
-        values = [jnp.where(chosen, moved_up(x, bit), x) for x in values]
-    return values
-
-
-def move_plan(has):
-    sub, lane = indices(has.shape)
-    empty = jnp.where(has, 0, 1)
-    ahead = empty
-    for step in (1, 2, 4):
-        ahead = ahead + jnp.where(sub >= step, pltpu.roll(ahead, step, 1), 0)
-    column = jnp.broadcast_to(ahead[:, 7:8, :], has.shape)
-    across = column
-    for step in (1, 2, 4, 8, 16, 32, 64):
-        across = across + jnp.where(lane >= step, pltpu.roll(across, step, 2), 0)
-    whole = jnp.broadcast_to(across[:, :, LANES - 1 :], has.shape)
-    sums = [jnp.zeros_like(whole[0])]
-    for block in range(has.shape[0] - 1):
-        sums.append(sums[-1] + whole[block])
-    distance = ahead - empty + across - column + jnp.stack(sums)
-    way = jnp.where(has, distance, 0)
-    starts = jnp.zeros_like(way)
-    ends = jnp.zeros_like(way)
-    for bit in range(BITS):
-        here = jnp.bitwise_and(way, 1 << bit)
-        starts = jnp.bitwise_or(starts, here)
+        here = [jnp.bitwise_and(x, 1 << bit) for x in way]
+        starts = [jnp.bitwise_or(x, h) for x, h in zip(starts, here)]
         coming = moved_down(way, bit)
-        arriving = jnp.bitwise_and(coming, 1 << bit)
-        ends = jnp.bitwise_or(ends, arriving)
-        way = jnp.where(arriving != 0, coming, jnp.where(here != 0, 0, way))
+        arriving = [jnp.bitwise_and(x, 1 << bit) for x in coming]
+        ends = [jnp.bitwise_or(x, a) for x, a in zip(ends, arriving)]
+        way = [
+            jnp.where(a != 0, y, jnp.where(h != 0, 0, x))
+            for a, y, h, x in zip(arriving, coming, here, way)
+        ]
     return starts, ends
 
 
@@ -166,6 +157,7 @@
     push_lists,
     leaving_mass,
     push,
+    weights,
     send_sems,
     ring_sems,
     home_sems,
@@ -223,15 +215,10 @@
         load.start()
     pl.semaphore_wait(barrier, n_phi + n_row - 2)
 
-    lane = lax.broadcasted_iota(jnp.int32, (n_phi, LANES), 1)
+    lane = lax.broadcasted_iota(jnp.int32, (8, LANES), 1)
     sub = lax.broadcasted_iota(jnp.int32, (8, LANES), 0)
     part = jnp.bitwise_and(sub, 3)
     even = jnp.bitwise_and(sub, 1) == 0
-
-    def far_first(i):
-        half = lax.shift_right_logical(i, 1)
-        ahead = jnp.where(jnp.bitwise_and(i, 1) == 1, n_phi // 2 + half, n_phi // 2 - half)
-        return lax.rem(me + ahead, n_phi)
 
     def to_ring(step, chunk, ring):
         landing = ring.at[pl.ds(me * RADIAL, RADIAL)]
@@ -290,55 +277,74 @@
             each(field, height, stay)
 
     def ring_wait(step, ring):
-        pltpu.make_async_copy(ring, ring, ring_sems.at[step]).wait()
-
-    def sweep(step, ring, swept):
-        def one(r, _):
-            x = ring[pl.ds(r, n_phi, stride=RADIAL), :]
-            offset = offsets[step, r]
-            hops = lax.shift_right_logical(offset, 7)
-            rest = jnp.bitwise_and(offset, 127)
-            x = pltpu.roll(x, hops, 0)
-            x = pltpu.roll(x, rest, 1)
-            x = jnp.where(lane >= rest, x, pltpu.roll(x, 1, 0))
-            before = pltpu.roll(x, 1, 0)
-            after = pltpu.roll(x, n_phi - 1, 0)
-
-            def back(k):
-                return pltpu.roll(jnp.where(lane < LANES - k, x, before), k, 1)
-
-            def ahead(k):
-                return pltpu.roll(jnp.where(lane >= k, x, after), LANES - k, 1)
-
-            m1, m2, m3 = back(1), back(2), back(3)
-            p1, p2, p3 = ahead(1), ahead(2), ahead(3)
-            c = jnp.full((n_phi, LANES), courants[step, r], jnp.float32)
+        circle = ring.at[pl.ds(0, n_phi * RADIAL)]
+        pltpu.make_async_copy(circle, circle, ring_sems.at[step]).wait()
+
+    def tap_weights():
+        def one(index, _):
+            step = lax.shift_right_logical(index, 4)
+            c = jnp.full((8, LANES), courants[step, jnp.bitwise_and(index, 15)], jnp.float32)
             size = jnp.abs(c)
-            upwind = c >= 0.0
-            f_m2 = face_value(m3, m2, m1, x)
-            f_m1 = face_value(m2, m1, x, p1)
-            f_0 = face_value(m1, x, p1, p2)
-            f_p1 = face_value(x, p1, p2, p3)
-            inner = 1.0 - size * (2.0 / 3.0)
-
-            def flux(face, low_face, high_face, low, high):
-                other = jnp.where(upwind, low_face, high_face)
-                base = jnp.where(upwind, low, high)
-                bend = 6.0 * base - 3.0 * (other + face)
-                return face - 0.5 * size * ((face - other) - inner * bend)
-
-            change = flux(f_0, f_m1, f_p1, x, p1) - flux(f_m1, f_m2, f_0, m1, x)
-            swept[pl.ds(r, n_phi, stride=RADIAL), :] = x - c * change
+            up = c >= 0.0
+            bend = 1.5 * size * (1.0 - size * (2.0 / 3.0))
+            face = c * (1.0 - 0.5 * size - bend) * twelfth
+            other = c * (0.5 * size - bend) * twelfth
+            cell = 2.0 * c * bend
+            other_up, cell_up = jnp.where(up, other, 0.0), jnp.where(up, cell, 0.0)
+            other_down, cell_down = other - other_up, cell - cell_up
+            taps = (
+                -other_up,
+                8.0 * other_up - face,
+                8.0 * face - other_down + cell_up,
+                1.0 - 8.0 * other_up + 8.0 * other_down - cell_up + cell_down,
+                other_up - 8.0 * face - cell_down,
+                face - 8.0 * other_down,
+                other_down,
+            )
+            for k in range(TAPS):
+                spot = pl.multiple_of((index * TAPS + k) * 8, 8)
+                weights[pl.ds(spot, 8), :] = taps[k]
             return 0
 
-        lax.fori_loop(0, RADIAL, one, 0, unroll=2)
-
-    def to_home(step, swept, home):
+        lax.fori_loop(0, STEPS * RADIAL, one, 0)
+
+    def sweep_and_send(step, ring, swept, home):
         landing = home.at[pl.ds(my_slab * SLAB + PAD, RADIAL)]
         arrival = home_sems.at[step * CHUNKS + my_chunk]
-
-        def send(i, _):
-            target = far_first(i)
+        my_group = lax.shift_right_logical(me, 3)
+        ring[pl.ds(n_phi * RADIAL, 8 * RADIAL), :] = ring[pl.ds(0, 8 * RADIAL), :]
+
+        def sweep(group):
+            def one(r, _):
+                offset = offsets[step, r]
+                first = 8 * group + n_phi - lax.shift_right_logical(offset, 7)
+                rest = jnp.bitwise_and(offset, LANES - 1)
+
+                def block(by):
+                    start = jnp.bitwise_and(first + by, n_phi - 1) * RADIAL + r
+                    return ring[pl.ds(start, 8, stride=RADIAL), :]
+
+                x = [block(by) for by in (-2, -1, 0, 1)]
+                inside = lane < LANES - rest
+                before, here, after = (
+                    pltpu.roll(jnp.where(inside, x[b + 1], x[b]), rest, 1) for b in range(3)
+                )
+
+                def weight(k):
+                    spot = pl.multiple_of(((step * RADIAL + r) * TAPS + k) * 8, 8)
+                    return weights[pl.ds(spot, 8), :]
+
+                total = weight(3) * here
+                for k in (1, 2, 3):
+                    back = pltpu.roll(jnp.where(lane < LANES - k, here, before), k, 1)
+                    ahead = pltpu.roll(jnp.where(lane >= k, here, after), LANES - k, 1)
+                    total = total + weight(3 - k) * back + weight(3 + k) * ahead
+                swept[pl.ds(group * 8 * RADIAL + r, 8, stride=RADIAL), :] = total
+                return 0
+
+            lax.fori_loop(0, RADIAL, one, 0, unroll=4)
+
+        def send(target):
             pltpu.make_async_remote_copy(
                 src_ref=swept.at[pl.ds(target * RADIAL, RADIAL)],
                 dst_ref=landing,
@@ -347,9 +353,26 @@
                 device_id={"phi": target},
                 device_id_type=MESH,
             ).start()
+
+        def away(index, _):
+            group = jnp.bitwise_and(my_group + jnp.where(index == 2, 1, 2 + index), 3)
+            sweep(group)
+
+            def each(j, _):
+                send(8 * group + jnp.bitwise_and(me + 4 + j, 7))
+                return 0
+
+            lax.fori_loop(0, 8, each, 0)
             return 0
 
-        lax.fori_loop(1, n_phi, send, 0)
+        lax.fori_loop(0, 3, away, 0)
+        sweep(my_group)
+
+        def near(j, _):
+            send(8 * my_group + jnp.bitwise_and(me + j, 7))
+            return 0
+
+        lax.fori_loop(1, 8, near, 0)
         pltpu.make_async_copy(swept.at[pl.ds(me * RADIAL, RADIAL)], landing, arrival).start()
 
     def home_wait(step, chunk):
@@ -491,9 +514,6 @@
             unroll=2,
         )
 
-    def blocks(value):
-        return value.reshape(slab_rows // 8, 8, LANES)
-
     def plan():
         def one(r, _):
             rows = pl.ds(r, nz, stride=RADIAL)
@@ -521,13 +541,26 @@
             return 0
 
         lax.fori_loop(0, RADIAL, one, 0)
-        has = blocks(move[...]) > 0
+        places = [pl.ds(8 * v, 8) for v in range(slab_rows // 8)]
+        has = [move[place, :] > 0 for place in places]
         starts, ends = move_plan(has)
-        picks[...] = ends.reshape(slab_rows, LANES)
-        marks = jnp.where(has, 1 << HAS_BIT, 0) + blocks(dest[...]) * (1 << DEST_BIT)
-        route[...] = jnp.bitwise_or(starts, marks).reshape(slab_rows, LANES)
-        (listed,) = compact([blocks(leaving_mass[...])], ends)
-        mass_list[...] = listed.reshape(LIST, LANES)
+        for place, h, start, end in zip(places, has, starts, ends):
+            marks = jnp.where(h, 1 << HAS_BIT, 0) + dest[place, :] * (1 << DEST_BIT)
+            picks[place, :] = end
+            route[place, :] = jnp.bitwise_or(start, marks)
+        mass_list[pl.ds(16, 8), :] = jnp.zeros((8, LANES), jnp.float32)
+        listed = compact([[leaving_mass[place, :] for place in places]])
+        store_list(mass_list, 0, listed[0])
+
+    def compact(values):
+        words = [picks[pl.ds(8 * v, 8), :] for v in range(slab_rows // 8)]
+        return chosen_moves(values, words, range(BITS), moved_down)
+
+    def store_list(ref, base, xs):
+        for v in range(16):
+            ref[pl.ds(base + v, 1), :] = xs[v][0:1]
+        for v in range(LIST - 16):
+            ref[pl.ds(base + 16 + v, 1), :] = xs[v][1:2]
 
     def table(j, values):
         value = jnp.int32(values[0])
@@ -580,21 +613,33 @@
             piece = landing.at[pl.ds(0, (n_row - 1) * source.shape[0])]
             pltpu.make_async_copy(piece, piece, sems.at[number]).wait()
 
-    def add(number, landing, count, source):
-        code = blocks(routes[pl.ds(source * slab_rows, slab_rows), :])
-        lists = [
-            landing[pl.ds((source * count + j) * LIST, LIST), :].reshape(LIST // 8, 8, LANES)
-            for j in range(count)
+    def add(number, landing, starts, source):
+        words = [
+            routes[pl.ds(pl.multiple_of(source * slab_rows + 8 * v, 8), 8), :]
+            for v in range(slab_rows // 8)
         ]
-        spread = expand(lists, code, slab_rows // 8)
-        wanted = lax.shift_right_logical(code, DEST_BIT) == tile + (1 << (HAS_BIT - DEST_BIT))
-        for j in range(count):
-            added = jnp.where(wanted, spread[j], 0.0).reshape(slab_rows, LANES)
-            grid[number + j] = grid[number + j] + added
+
+        def first(start, v):
+            def row(index):
+                return jnp.broadcast_to(landing[pl.ds(start + index, 1), :], (8, LANES))
+
+            return jnp.where(sub == 1, row(16 + v), row(v)) if v < LIST - 16 else row(v)
+
+        lists = [[first(start, v) for v in range(16)] for start in starts]
+        spread = chosen_moves(lists, words, reversed(range(BITS)), moved_up)
+        for v in range(16):
+            wanted = lax.shift_right_logical(words[v], DEST_BIT) == tile + (
+                1 << (HAS_BIT - DEST_BIT)
+            )
+            for j in range(len(starts)):
+                place = pl.ds(8 * v, 8)
+                added = jnp.where(wanted, spread[j][v], 0.0)
+                grid[number + j, place, :] = grid[number + j, place, :] + added
 
     def gather_mass():
         def one(i, _):
-            add(0, mass_lists, 1, lax.rem(tile + i, n_row))
+            source = lax.rem(tile + i, n_row)
+            add(0, mass_lists, [source * MASS_ROWS], source)
             return 0
 
         lax.fori_loop(1, n_row, one, 0)
@@ -603,7 +648,8 @@
         def one(j, _):
             source = neighbour(j, -1)
             push_copy(j, source).wait_recv()
-            add(1, push_lists, 2, source)
+            base = source * 2 * LIST
+            add(1, push_lists, [base, base + LIST], source)
             return 0
 
         lax.fori_loop(0, n_row - 1, one, 0)
@@ -614,12 +660,12 @@
         to_ring(0, chunk, ring_a)
     for load in loads:
         load.wait()
+    tap_weights()
     plan()
     to_tiles(early)
     for step, ring, swept, home in ((0, ring_a, swept_a, home_a), (1, ring_b, swept_b, home_b)):
         ring_wait(step, ring)
-        sweep(step, ring, swept)
-        to_home(step, swept, home)
+        sweep_and_send(step, ring, swept, home)
         if step == 1:
             tiles_wait(early, list_sems)
             gather_mass()
@@ -632,9 +678,14 @@
             if step + 1 < STEPS:
                 to_ring(step + 1, chunk, ring_b)
     parted = push.reshape(nz, FIELDS, RADIAL, LANES)
-    pushes = compact([blocks(parted[:, 2]), blocks(parted[:, 3])], blocks(picks[...]))
-    push_list[pl.ds(0, LIST), :] = pushes[0].reshape(LIST, LANES)
-    push_list[pl.ds(LIST, LIST), :] = pushes[1].reshape(LIST, LANES)
+    pushes = compact(
+        [
+            [parted[v // 2, quantity, 8 * (v % 2) : 8 * (v % 2) + 8] for v in range(16)]
+            for quantity in (2, 3)
+        ]
+    )
+    for j in range(2):
+        store_list(push_list, j * LIST, pushes[j])
     push_start()
     grid[1] = parted[:, 0].reshape(slab_rows, LANES)
     grid[2] = parted[:, 1].reshape(slab_rows, LANES)
@@ -689,8 +740,8 @@
         in_specs=[hbm, hbm, smem, smem] + [hbm] * 6,
         out_specs=[vmem] * 2,
         scratch_shapes=[
-            rows(ring),
-            rows(ring),
+            rows(ring + 8 * radial),
+            rows(ring + 8 * radial),
             rows(ring),
             rows(ring),
             rows(FIELDS * nz * SLAB),
@@ -710,12 +761,13 @@
             rows(cells, jnp.int32),
             rows(cells, jnp.int32),
             rows(n_row * cells, jnp.int32),
-            rows(LIST),
-            rows(n_row * LIST),
+            rows(MASS_ROWS),
+            rows(n_row * MASS_ROWS),
             rows(2 * LIST),
             rows(2 * n_row * LIST),
             rows(cells),
             rows(FIELDS * cells),
+            rows(STEPS * radial * TAPS * 8),
             dma((2 * STEPS,)),
             dma((STEPS,)),
             dma((STEPS * CHUNKS,)),

time: 67.4 us -> 65.6 us (0.973)
  Pallas kernels: 66.5 us -> 64.9 us
    pallas_call x1, Pallas kernels: 65.7 us -> 64.1 us  [gas_and_dust(): pl.pallas_call(functools.partial(gas_kernel, n_phi, n_row, nz), out_shape...]
where the time goes in v6:
time: 65.6 us; the launch traced here: 65.5 us
  Pallas kernels  64.9 us (99%)
    pallas_call x1, Pallas kernels, gas_and_dust(): pl.pallas_call(functools.partial(gas_kernel, n_phi, n_row, nz), out_shape...  64.1 us

profile of v6, /device:TPU:8, one launch (start us, length us, event | category | flops | bytes accessed | tf_op | source)
XLA Modules:
  0.0 65.5 jit_solution(12859407234286561230)
XLA Ops:
  0.6 64.1 %shard_map.121 = (f32[512,128]{1,0:T(8,128)S(1)}, f32[3,128,128]{2,1,0:T(8,128)S(1)}) custom-call(f32[128,128]{1,0:T(8,128)} %bitcast.16, f32[384,128]{1,0:T(8,128)} %bitcast.15, s32[2,16]{1,0:T(2,128)} %offsets.1, f32[2,16]{1,0:T(2,128)} %courants.1, f32[512,128]{1,0:T(8,128)} %bitcast.13, f32[512,128]{1,0:T(8,128)} %bitcast.14, f32[1024,128]{1,0:T(8,128)} %bitcast.12, ...), custom_call_target="tpu_custom_call" | custom-call | tf_op jit(solution)/shard_map/pallas_call | solution.py:734
  64.7 0.8 %shard_map.122 = (f32[8,16,128]{2,1,0:T(8,128)}, f32[3,8,16,128]{3,2,1,0:T(8,128)}, f32[3,8,16,128]{3,2,1,0:T(8,128)}) custom-call(f32[8,4,16,128]{3,2,1,0:T(8,128)S(1)} %bitcast.10, f32[3,8,16,128]{3,2,1,0:T(8,128)S(1)} %bitcast.11), custom_call_target="tpu_custom_call" | custom-call | tf_op jit(solution)/shard_map/pallas_call | solution.py:797

commit v7 on v6

--- a/solution.py
+++ b/solution.py
@@ -21,10 +21,12 @@
 LIST = 20
 MASS_ROWS = 24
 TAPS = 7
-DEST_BIT = 14
-HAS_BIT = 17
+ROW_BIT = 12
+DEST_BIT = 17
+HAS_BIT = 20
 BITS = 14
 CHUNKS = 4
+IN_BOUNDS = "promise_in_bounds"
 VMEM_BYTES = 56 * 1024 * 1024
 COPY_VMEM_BYTES = 2 * 1024 * 1024
 MESH = pl.DeviceIdType.MESH
@@ -50,22 +52,6 @@
     after = xs[1:] + [pltpu.roll(xs[0], 7, 0)]
     return [
         pltpu.roll(jnp.where(lane < step, after[v], xs[v]), LANES - step, 1) for v in range(count)
-    ]
-
-
-def moved_up(xs, bit):
-    count = len(xs)
-    if bit >= 11:
-        return [pltpu.roll(x, 1 << (bit - 11), 0) for x in xs]
-    if bit >= 7:
-        step = 1 << (bit - 7)
-        return [pltpu.roll(x, 1, 0) for x in xs[count - step :]] + xs[: count - step]
-    step = 1 << bit
-    lane = lanes_of(xs[0])
-    before = [pltpu.roll(xs[-1], 1, 0)] + xs[:-1]
-    return [
-        pltpu.roll(jnp.where(lane >= LANES - step, before[v], xs[v]), step, 1)
-        for v in range(count)
     ]
 
 
@@ -96,14 +82,17 @@
     for step in (1, 2, 4):
         whole = whole + jnp.where(sub >= step, pltpu.roll(whole, step, 0), 0)
     whole = whole - sums[-1]
+    starts = [8 * LANES * 2 * sub + LANES * v - sums[v] - whole for v in range(len(has))]
+    codes = [
+        start + lane - x + e + lax.shift_left(lax.shift_right_logical(start, 7), ROW_BIT)
+        for start, x, e in zip(starts, ahead, empty)
+    ]
     way = [
         jnp.where(h, x - e + total + whole, 0) for h, x, e, total in zip(has, ahead, empty, sums)
     ]
-    starts = [jnp.zeros_like(x) for x in way]
-    ends = starts
+    ends = [jnp.zeros_like(x) for x in way]
     for bit in range(BITS):
         here = [jnp.bitwise_and(x, 1 << bit) for x in way]
-        starts = [jnp.bitwise_or(x, h) for x, h in zip(starts, here)]
         coming = moved_down(way, bit)
         arriving = [jnp.bitwise_and(x, 1 << bit) for x in coming]
         ends = [jnp.bitwise_or(x, a) for x, a in zip(ends, arriving)]
@@ -111,7 +100,7 @@
             jnp.where(a != 0, y, jnp.where(h != 0, 0, x))
             for a, y, h, x in zip(arriving, coming, here, way)
         ]
-    return starts, ends
+    return codes, ends
 
 
 def gas_kernel(
@@ -543,11 +532,11 @@
         lax.fori_loop(0, RADIAL, one, 0)
         places = [pl.ds(8 * v, 8) for v in range(slab_rows // 8)]
         has = [move[place, :] > 0 for place in places]
-        starts, ends = move_plan(has)
-        for place, h, start, end in zip(places, has, starts, ends):
+        codes, ends = move_plan(has)
+        for place, h, code, end in zip(places, has, codes, ends):
             marks = jnp.where(h, 1 << HAS_BIT, 0) + dest[place, :] * (1 << DEST_BIT)
             picks[place, :] = end
-            route[place, :] = jnp.bitwise_or(start, marks)
+            route[place, :] = jnp.bitwise_or(code, marks)
         mass_list[pl.ds(16, 8), :] = jnp.zeros((8, LANES), jnp.float32)
         listed = compact([[leaving_mass[place, :] for place in places]])
         store_list(mass_list, 0, listed[0])
@@ -591,55 +580,79 @@
 
         lax.fori_loop(0, n_row - 1, send, 0)
 
-    def to_tiles(pairs):
-        def send(i, _):
-            target = lax.rem(tile + i, n_row)
-            for number, source, landing in pairs:
-                count = source.shape[0]
-                pltpu.make_async_remote_copy(
-                    src_ref=source,
-                    dst_ref=landing.at[pl.ds(tile * count, count)],
-                    send_sem=list_send_sems.at[number],
-                    recv_sem=list_sems.at[number],
-                    device_id={"row": target},
-                    device_id_type=MESH,
-                ).start()
+    across = jnp.bitwise_xor(tile, 1)
+
+    def slot(landing, index):
+        count = landing.shape[0] // n_row
+        return landing.at[pl.ds(pl.multiple_of(index * count, 8), count)]
+
+    def plan_copy(source, target_slot, number, target):
+        return pltpu.make_async_remote_copy(
+            src_ref=source,
+            dst_ref=target_slot,
+            send_sem=list_send_sems.at[number],
+            recv_sem=list_sems.at[number],
+            device_id={"row": target},
+            device_id_type=MESH,
+        )
+
+    def plan_across():
+        return [
+            plan_copy(source, slot(landing, tile), number, across)
+            for number, source, landing in ((0, route, routes), (1, mass_list, mass_lists))
+        ]
+
+    def plan_along():
+        for copy in plan_across():
+            copy.wait_recv()
+
+        def send(step, _):
+            target = jnp.bitwise_and(tile + 2 * step, n_row - 1)
+            for number, source, landing in ((2, route, routes), (3, mass_list, mass_lists)):
+                plan_copy(source, slot(landing, tile), number, target).start()
+                theirs = slot(landing, across)
+                plan_copy(theirs, theirs, number, target).start()
             return 0
 
-        lax.fori_loop(1, n_row, send, 0)
-
-    def tiles_wait(pairs, sems):
-        for number, source, landing in pairs:
-            piece = landing.at[pl.ds(0, (n_row - 1) * source.shape[0])]
+        lax.fori_loop(1, n_row // 2, send, 0)
+
+    def plan_wait(sems):
+        for number, landing in ((2, routes), (3, mass_lists)):
+            piece = landing.at[pl.ds(0, (n_row - 2) * (landing.shape[0] // n_row))]
             pltpu.make_async_copy(piece, piece, sems.at[number]).wait()
 
-    def add(number, landing, starts, source):
-        words = [
-            routes[pl.ds(pl.multiple_of(source * slab_rows + 8 * v, 8), 8), :]
-            for v in range(slab_rows // 8)
-        ]
-
-        def first(start, v):
-            def row(index):
-                return jnp.broadcast_to(landing[pl.ds(start + index, 1), :], (8, LANES))
-
-            return jnp.where(sub == 1, row(16 + v), row(v)) if v < LIST - 16 else row(v)
-
-        lists = [[first(start, v) for v in range(16)] for start in starts]
-        spread = chosen_moves(lists, words, reversed(range(BITS)), moved_up)
-        for v in range(16):
-            wanted = lax.shift_right_logical(words[v], DEST_BIT) == tile + (
-                1 << (HAS_BIT - DEST_BIT)
+    def add(number, landing, base, firsts, source):
+        def rows(m):
+            return landing[pl.ds(pl.multiple_of(base + 8 * m, 8), 8), :]
+
+        held = [rows(m) for m in range(firsts[-1] // 8 + 3)]
+
+        def one_row(index, low):
+            place = jnp.bitwise_and(index, 7)
+            block = lax.shift_right_logical(index, 3)
+            found = [jnp.take_along_axis(held[low + m], place, axis=0, mode=IN_BOUNDS) for m in range(3)]
+            return jnp.where(
+                block == low, found[0], jnp.where(block == low + 1, found[1], found[2])
             )
-            for j in range(len(starts)):
-                place = pl.ds(8 * v, 8)
-                added = jnp.where(wanted, spread[j][v], 0.0)
+
+        for v in range(slab_rows // 8):
+            word = routes[pl.ds(pl.multiple_of(source * slab_rows + 8 * v, 8), 8), :]
+            spot = jnp.bitwise_and(word, LANES - 1)
+            row = jnp.bitwise_and(lax.shift_right_logical(word, ROW_BIT), 31)
+            same = jnp.bitwise_and(lax.shift_right_logical(word, 7), 31) == row
+            wanted = lax.shift_right_logical(word, DEST_BIT) == tile + (1 << (HAS_BIT - DEST_BIT))
+            place = pl.ds(8 * v, 8)
+            for j, first in enumerate(firsts):
+                near = jnp.take_along_axis(one_row(row + first, first // 8), spot, axis=1, mode=IN_BOUNDS)
+                next_row = one_row(row + (first + 1), first // 8)
+                far = jnp.take_along_axis(next_row, spot, axis=1, mode=IN_BOUNDS)
+                added = jnp.where(wanted, jnp.where(same, near, far), 0.0)
                 grid[number + j, place, :] = grid[number + j, place, :] + added
 
     def gather_mass():
         def one(i, _):
             source = lax.rem(tile + i, n_row)
-            add(0, mass_lists, [source * MASS_ROWS], source)
+            add(0, mass_lists, source * MASS_ROWS, (0,), source)
             return 0
 
         lax.fori_loop(1, n_row, one, 0)
@@ -648,30 +661,32 @@
         def one(j, _):
             source = neighbour(j, -1)
             push_copy(j, source).wait_recv()
-            base = source * 2 * LIST
-            add(1, push_lists, [base, base + LIST], source)
+            add(1, push_lists, source * 2 * LIST, (0, LIST), source)
             return 0
 
         lax.fori_loop(0, n_row - 1, one, 0)
 
-    early = ((0, route, routes), (1, mass_list, mass_lists))
-
-    for chunk in range(CHUNKS):
-        to_ring(0, chunk, ring_a)
+    to_ring(0, 0, ring_a)
+    to_ring(0, 1, ring_a)
     for load in loads:
         load.wait()
     tap_weights()
     plan()
-    to_tiles(early)
+    to_ring(0, 2, ring_a)
+    to_ring(0, 3, ring_a)
+    for copy in plan_across():
+        copy.start()
     for step, ring, swept, home in ((0, ring_a, swept_a, home_a), (1, ring_b, swept_b, home_b)):
         ring_wait(step, ring)
         sweep_and_send(step, ring, swept, home)
         if step == 1:
-            tiles_wait(early, list_sems)
+            plan_wait(list_sems)
             gather_mass()
         for chunk in range(CHUNKS):
             home_wait(step, chunk)
             rims_start(step, chunk, home)
+        if step == 0:
+            plan_along()
         for chunk in range(CHUNKS):
             rims_wait(step, chunk, home)
             finish(step, chunk, home)
@@ -690,7 +705,9 @@
     grid[1] = parted[:, 0].reshape(slab_rows, LANES)
     grid[2] = parted[:, 1].reshape(slab_rows, LANES)
     gather_push()
-    tiles_wait(early, list_send_sems)
+    for copy in plan_across():
+        copy.wait_send()
+    plan_wait(list_send_sems)
     sent = push_lists.at[pl.ds(0, (n_row - 1) * 2 * LIST)]
     pltpu.make_async_copy(sent, sent, push_send_sem.at[0]).wait()
     partners = (n_phi - 1) * RADIAL
@@ -773,8 +790,8 @@
             dma((STEPS * CHUNKS,)),
             dma((2 * STEPS * CHUNKS,)),
             dma((2 * STEPS * CHUNKS,)),
-            dma((2,)),
-            dma((2,)),
+            dma((4,)),
+            dma((4,)),
             dma((1,)),
             dma((n_row - 1,)),
             dma((6,)),

time: 65.6 us -> 61.5 us (0.938); the launches traced: 65.5 us -> 60.7 us
  Pallas kernels: 64.9 us -> 60.1 us
    pallas_call x1, Pallas kernels: 64.1 us -> 59.3 us  [gas_and_dust(): pl.pallas_call(functools.partial(gas_kernel, n_phi, n_row, nz), out_shape...]
where the time goes in v7:
time: 61.5 us; the launch traced here: 60.7 us
  Pallas kernels  60.1 us (98%)
  between operations  0.64 us (1%)
    pallas_call x1, Pallas kernels, gas_and_dust(): pl.pallas_call(functools.partial(gas_kernel, n_phi, n_row, nz), out_shape...  59.3 us

profile of v7, /device:TPU:8, one launch (start us, length us, event | category | flops | bytes accessed | tf_op | source)
XLA Modules:
  0.0 60.7 jit_solution(17757942246440530427)
XLA Ops:
  0.6 59.3 %shard_map.121 = (f32[512,128]{1,0:T(8,128)S(1)}, f32[3,128,128]{2,1,0:T(8,128)S(1)}) custom-call(f32[128,128]{1,0:T(8,128)} %bitcast.16, f32[384,128]{1,0:T(8,128)} %bitcast.15, s32[2,16]{1,0:T(2,128)} %offsets.1, f32[2,16]{1,0:T(2,128)} %courants.1, f32[512,128]{1,0:T(8,128)} %bitcast.13, f32[512,128]{1,0:T(8,128)} %bitcast.14, f32[1024,128]{1,0:T(8,128)} %bitcast.12, ...), custom_call_target="tpu_custom_call" | custom-call | tf_op jit(solution)/shard_map/pallas_call | solution.py:751
  59.9 0.8 %shard_map.122 = (f32[8,16,128]{2,1,0:T(8,128)}, f32[3,8,16,128]{3,2,1,0:T(8,128)}, f32[3,8,16,128]{3,2,1,0:T(8,128)}) custom-call(f32[8,4,16,128]{3,2,1,0:T(8,128)S(1)} %bitcast.10, f32[3,8,16,128]{3,2,1,0:T(8,128)S(1)} %bitcast.11), custom_call_target="tpu_custom_call" | custom-call | tf_op jit(solution)/shard_map/pallas_call | solution.py:814

commit v8 on v7

--- a/solution.py
+++ b/solution.py
@@ -188,18 +188,18 @@
 
     def greet(i, _):
         pl.semaphore_signal(
-            barrier, inc=1, device_id={"phi": lax.rem(me + i, n_phi)}, device_id_type=MESH
+            barrier, inc=1, device_id={"phi": jnp.bitwise_and(me + i, n_phi - 1)}, device_id_type=MESH
         )
         return 0
 
     def greet_row(i, _):
         pl.semaphore_signal(
-            barrier, inc=1, device_id={"row": lax.rem(tile + i, n_row)}, device_id_type=MESH
+            barrier, inc=1, device_id={"row": jnp.bitwise_and(tile + i, n_row - 1)}, device_id_type=MESH
         )
         return 0
 
-    lax.fori_loop(1, n_phi, greet, 0)
-    lax.fori_loop(1, n_row, greet_row, 0)
+    lax.fori_loop(1, n_phi, greet, 0, unroll=n_phi - 1)
+    lax.fori_loop(1, n_row, greet_row, 0, unroll=n_row - 1)
     for load in loads:
         load.start()
     pl.semaphore_wait(barrier, n_phi + n_row - 2)
@@ -331,7 +331,7 @@
                 swept[pl.ds(group * 8 * RADIAL + r, 8, stride=RADIAL), :] = total
                 return 0
 
-            lax.fori_loop(0, RADIAL, one, 0, unroll=4)
+            lax.fori_loop(0, RADIAL, one, 0, unroll=16)
 
         def send(target):
             pltpu.make_async_remote_copy(
@@ -500,7 +500,7 @@
             RADIAL,
             one,
             (first, face_1, face_2, start[3], start[4], start[5], speed_1),
-            unroll=2,
+            unroll=4,
         )
 
     def plan():
@@ -630,7 +630,10 @@
         def one_row(index, low):
             place = jnp.bitwise_and(index, 7)
             block = lax.shift_right_logical(index, 3)
-            found = [jnp.take_along_axis(held[low + m], place, axis=0, mode=IN_BOUNDS) for m in range(3)]
+            found = [
+                jnp.take_along_axis(held[low + m], place, axis=0, mode=IN_BOUNDS)
+                for m in range(3)
+            ]
             return jnp.where(
                 block == low, found[0], jnp.where(block == low + 1, found[1], found[2])
             )
@@ -685,13 +688,13 @@
         for chunk in range(CHUNKS):
             home_wait(step, chunk)
             rims_start(step, chunk, home)
-        if step == 0:
-            plan_along()
         for chunk in range(CHUNKS):
             rims_wait(step, chunk, home)
             finish(step, chunk, home)
             if step + 1 < STEPS:
                 to_ring(step + 1, chunk, ring_b)
+        if step == 0:
+            plan_along()
     parted = push.reshape(nz, FIELDS, RADIAL, LANES)
     pushes = compact(
         [

time: 61.5 us -> 58.2 us (0.946)
  Pallas kernels: 60.1 us -> 57.3 us
    pallas_call x1, Pallas kernels: 59.3 us -> 56.5 us  [gas_and_dust(): pl.pallas_call(functools.partial(gas_kernel, n_phi, n_row, nz), out_shape...]
where the time goes in v8:
time: 58.2 us; the launch traced here: 57.9 us
  Pallas kernels  57.3 us (98%)
  between operations  0.64 us (1%)
    pallas_call x1, Pallas kernels, gas_and_dust(): pl.pallas_call(functools.partial(gas_kernel, n_phi, n_row, nz), out_shape...  56.5 us

profile of v8, /device:TPU:8, one launch (start us, length us, event | category | flops | bytes accessed | tf_op | source)
XLA Modules:
  0.0 57.9 jit_solution(11849014749283181861)
XLA Ops:
  0.6 56.5 %shard_map.121 = (f32[512,128]{1,0:T(8,128)S(1)}, f32[3,128,128]{2,1,0:T(8,128)S(1)}) custom-call(f32[128,128]{1,0:T(8,128)} %bitcast.16, f32[384,128]{1,0:T(8,128)} %bitcast.15, s32[2,16]{1,0:T(2,128)} %offsets.1, f32[2,16]{1,0:T(2,128)} %courants.1, f32[512,128]{1,0:T(8,128)} %bitcast.13, f32[512,128]{1,0:T(8,128)} %bitcast.14, f32[1024,128]{1,0:T(8,128)} %bitcast.12, ...), custom_call_target="tpu_custom_call" | custom-call | tf_op jit(solution)/shard_map/pallas_call | solution.py:754
  57.1 0.8 %shard_map.122 = (f32[8,16,128]{2,1,0:T(8,128)}, f32[3,8,16,128]{3,2,1,0:T(8,128)}, f32[3,8,16,128]{3,2,1,0:T(8,128)}) custom-call(f32[8,4,16,128]{3,2,1,0:T(8,128)S(1)} %bitcast.10, f32[3,8,16,128]{3,2,1,0:T(8,128)S(1)} %bitcast.11), custom_call_target="tpu_custom_call" | custom-call | tf_op jit(solution)/shard_map/pallas_call | solution.py:817

commit v9 on v8

--- a/solution.py
+++ b/solution.py
@@ -578,7 +578,7 @@
             push_copy(j, neighbour(j, 1)).start()
             return 0
 
-        lax.fori_loop(0, n_row - 1, send, 0)
+        lax.fori_loop(0, n_row - 1, send, 0, unroll=n_row - 1)
 
     across = jnp.bitwise_xor(tile, 1)
 
@@ -667,7 +667,7 @@
             add(1, push_lists, source * 2 * LIST, (0, LIST), source)
             return 0
 
-        lax.fori_loop(0, n_row - 1, one, 0)
+        lax.fori_loop(0, n_row - 1, one, 0, unroll=n_row - 1)
 
     to_ring(0, 0, ring_a)
     to_ring(0, 1, ring_a)
@@ -682,9 +682,6 @@
     for step, ring, swept, home in ((0, ring_a, swept_a, home_a), (1, ring_b, swept_b, home_b)):
         ring_wait(step, ring)
         sweep_and_send(step, ring, swept, home)
-        if step == 1:
-            plan_wait(list_sems)
-            gather_mass()
         for chunk in range(CHUNKS):
             home_wait(step, chunk)
             rims_start(step, chunk, home)
@@ -693,8 +690,8 @@
             finish(step, chunk, home)
             if step + 1 < STEPS:
                 to_ring(step + 1, chunk, ring_b)
-        if step == 0:
-            plan_along()
+            if step == 0 and chunk == 1:
+                plan_along()
     parted = push.reshape(nz, FIELDS, RADIAL, LANES)
     pushes = compact(
         [
@@ -705,6 +702,8 @@
     for j in range(2):
         store_list(push_list, j * LIST, pushes[j])
     push_start()
+    plan_wait(list_sems)
+    gather_mass()
     grid[1] = parted[:, 0].reshape(slab_rows, LANES)
     grid[2] = parted[:, 1].reshape(slab_rows, LANES)
     gather_push()

time: 58.2 us -> 58.1 us (level)
  no operation moved by 1% of the time
where the time goes in v9:
time: 58.1 us; the launch traced here: 57.8 us
  Pallas kernels  57.2 us (98%)
  between operations  0.64 us (1%)
    pallas_call x1, Pallas kernels, gas_and_dust(): pl.pallas_call(functools.partial(gas_kernel, n_phi, n_row, nz), out_shape...  56.4 us

profile of v9, /device:TPU:8, one launch (start us, length us, event | category | flops | bytes accessed | tf_op | source)
XLA Modules:
  0.0 57.8 jit_solution(10483880502769181452)
XLA Ops:
  0.6 56.4 %shard_map.121 = (f32[512,128]{1,0:T(8,128)S(1)}, f32[3,128,128]{2,1,0:T(8,128)S(1)}) custom-call(f32[128,128]{1,0:T(8,128)} %bitcast.16, f32[384,128]{1,0:T(8,128)} %bitcast.15, s32[2,16]{1,0:T(2,128)} %offsets.1, f32[2,16]{1,0:T(2,128)} %courants.1, f32[512,128]{1,0:T(8,128)} %bitcast.13, f32[512,128]{1,0:T(8,128)} %bitcast.14, f32[1024,128]{1,0:T(8,128)} %bitcast.12, ...), custom_call_target="tpu_custom_call" | custom-call | tf_op jit(solution)/shard_map/pallas_call | solution.py:753
  57.0 0.8 %shard_map.122 = (f32[8,16,128]{2,1,0:T(8,128)}, f32[3,8,16,128]{3,2,1,0:T(8,128)}, f32[3,8,16,128]{3,2,1,0:T(8,128)}) custom-call(f32[8,4,16,128]{3,2,1,0:T(8,128)S(1)} %bitcast.10, f32[3,8,16,128]{3,2,1,0:T(8,128)S(1)} %bitcast.11), custom_call_target="tpu_custom_call" | custom-call | tf_op jit(solution)/shard_map/pallas_call | solution.py:816

commit v10 on v9

--- a/solution.py
+++ b/solution.py
@@ -125,6 +125,7 @@
     swept_b,
     home_a,
     home_b,
+    fresh,
     leave,
     mass,
     stop,
@@ -184,6 +185,19 @@
         )
     ]
 
+    fields = fresh.reshape(nz, FIELDS, RADIAL, LANES)
+    speeds = velocity.reshape(FIELDS - 1, nz, RADIAL, LANES)
+    gas_loads = [
+        pltpu.make_async_copy(
+            density.reshape(nz, RADIAL, LANES), fields.at[:, 0], load_sems.at[len(loads)]
+        )
+    ] + [
+        pltpu.make_async_copy(speeds.at[f], fields.at[:, 1 + f], load_sems.at[len(loads) + 1 + f])
+        for f in range(FIELDS - 1)
+    ]
+    for load in gas_loads:
+        load.start()
+
     barrier = pltpu.get_barrier_semaphore()
 
     def greet(i, _):
@@ -202,6 +216,8 @@
     lax.fori_loop(1, n_row, greet_row, 0, unroll=n_row - 1)
     for load in loads:
         load.start()
+    for load in gas_loads:
+        load.wait()
     pl.semaphore_wait(barrier, n_phi + n_row - 2)
 
     lane = lax.broadcasted_iota(jnp.int32, (8, LANES), 1)
@@ -233,25 +249,14 @@
             target = (2 * field + chunk % 2) * 4 + 2 * side + chunk // 2
             return field, 2 * chunk + side, target
 
-        def rows(ref, index):
-            return ref.at[pl.ds(index * RADIAL, RADIAL)]
-
-        def each(field, height, act):
-            if step == 0:
-
-                @pl.when(field == 0)
-                def _():
-                    act(rows(density, height))
-
-                @pl.when(field > 0)
-                def _():
-                    act(rows(velocity, (field - 1) * nz + height))
-            else:
-                act(rows(leave, height * FIELDS + field))
+        gas = fresh if step == 0 else leave
+
+        def source(field, height):
+            return gas.at[pl.ds((height * FIELDS + field) * RADIAL, RADIAL)]
 
         def send(j, _):
             field, height, target = place(j)
-            each(field, height, lambda source: go(source, target))
+            go(source(field, height), target)
             return 0
 
         lax.fori_loop(0, 7, send, 0)
@@ -263,7 +268,7 @@
         @pl.when(my_chunk == chunk)
         def _():
             field, height, _unused = place(jnp.int32(7))
-            each(field, height, stay)
+            stay(source(field, height))
 
     def ring_wait(step, ring):
         circle = ring.at[pl.ds(0, n_phi * RADIAL)]
@@ -500,7 +505,7 @@
             RADIAL,
             one,
             (first, face_1, face_2, start[3], start[4], start[5], speed_1),
-            unroll=4,
+            unroll=16,
         )
 
     def plan():
@@ -766,6 +771,7 @@
             rows(FIELDS * nz * SLAB),
             rows(FIELDS * nz * SLAB),
             rows(FIELDS * cells),
+            rows(FIELDS * cells),
             rows(K * cells),
             rows(K * cells),
             rows(2 * K * cells),
@@ -796,7 +802,7 @@
             dma((4,)),
             dma((1,)),
             dma((n_row - 1,)),
-            dma((6,)),
+            dma((6 + FIELDS,)),
         ],
         compiler_params=pltpu.CompilerParams(
             collective_id=0, has_side_effects=True, vmem_limit_bytes=VMEM_BYTES

time: 58.1 us -> 58.1 us (level)
  no operation moved by 1% of the time
where the time goes in v10:
time: 58.1 us; the launch traced here: 57.5 us
  Pallas kernels  56.8 us (98%)
  between operations  0.64 us (1%)
    pallas_call x1, Pallas kernels, gas_and_dust(): pl.pallas_call(functools.partial(gas_kernel, n_phi, n_row, nz), out_shape...  56 us

profile of v10, /device:TPU:8, one launch (start us, length us, event | category | flops | bytes accessed | tf_op | source)
XLA Modules:
  0.0 57.5 jit_solution(7210677169966473498)
XLA Ops:
  0.6 56.0 %shard_map.121 = (f32[512,128]{1,0:T(8,128)S(1)}, f32[3,128,128]{2,1,0:T(8,128)S(1)}) custom-call(f32[128,128]{1,0:T(8,128)} %bitcast.16, f32[384,128]{1,0:T(8,128)} %bitcast.15, s32[2,16]{1,0:T(2,128)} %offsets.1, f32[2,16]{1,0:T(2,128)} %courants.1, f32[512,128]{1,0:T(8,128)} %bitcast.13, f32[512,128]{1,0:T(8,128)} %bitcast.14, f32[1024,128]{1,0:T(8,128)} %bitcast.12, ...), custom_call_target="tpu_custom_call" | custom-call | tf_op jit(solution)/shard_map/pallas_call | solution.py:758
  56.7 0.8 %shard_map.122 = (f32[8,16,128]{2,1,0:T(8,128)}, f32[3,8,16,128]{3,2,1,0:T(8,128)}, f32[3,8,16,128]{3,2,1,0:T(8,128)}) custom-call(f32[8,4,16,128]{3,2,1,0:T(8,128)S(1)} %bitcast.10, f32[3,8,16,128]{3,2,1,0:T(8,128)S(1)} %bitcast.11), custom_call_target="tpu_custom_call" | custom-call | tf_op jit(solution)/shard_map/pallas_call | solution.py:822
